TPU v7x, 256 devices: a whole 4x4x8 slice. The times are simulated.
256 devices in a mesh: dom: 32 (over y, z), sub: 8 (over x, core).
Axes of the slice: x: 4, y: 4, z: 8, core: 2. Of those that a mesh axis runs over, the one named last changes fastest.
Arguments:
- velocity: float32 [3, 216, 32768], P(None, None, ('dom', 'sub')), may hold values from -5 to 5
- base_flow: float32 [3, 216, 32768], P(None, None, ('dom', 'sub')), may hold values from -1.5 to 1.5
- viscosity: float32 [216, 32768], P(None, ('dom', 'sub')), may hold values from 0.05 to 1
- cell_order: int32 [256, 128], P(('dom', 'sub')), may hold values from 0 to 127, each once within a row
- coarse_inv: float32 [256, 256], replicated, as said below
Outputs:
- linearized: float32 [3, 216, 32768], P(None, None, ('dom', 'sub'))
- pressure: float32 [216, 32768], P(None, ('dom', 'sub'))
Inputs may be any that keep to these rules, and one draw needn't show every extreme that they name: `cell_order`: row d gives, for each of the 128 element slots of block d in order, that element's cell within the block; each cell once. `coarse_inv`: symmetric positive definite.
All inputs are finite; a program needn't handle non-finite values.
Results may differ from a plain program's by a relative error of at most 0.0003.
Values sent between devices are 32-bit elements; how exact they have to be, the bound alone decides.
A program may use at most 64 MiB of HBM per device.

v0:
```python
import jax
import jax.numpy as jnp
import numpy as np
from jax import lax
from jax.sharding import PartitionSpec as P

ELX = 2
ELY = 2
ELZ = 32
ITERS = 3


PRECISE = lax.Precision.HIGHEST
REACTION = 0.001


def extended(cells, sides, width):
    for axis, dim in sides:
        count = lax.axis_size(axis)
        ends = count - 1
        head = lax.slice_in_dim(cells, 0, width, axis=dim)
        tail = lax.slice_in_dim(cells, cells.shape[dim] - width, cells.shape[dim], axis=dim)
        cells = jnp.concatenate(
            [
                lax.ppermute(tail, axis, [(i, (i + 1) % count) for i in range(ends)]),
                cells,
                lax.ppermute(head, axis, [((i + 1) % count, i) for i in range(ends)]),
            ],
            axis=dim,
        )
    return cells


def gll_tables():
    gll_points = np.array(
        [
            -1.0,
            -0.7650553239294647,
            -0.2852315164806451,
            0.2852315164806451,
            0.7650553239294647,
            1.0,
        ]
    )
    gll_weights = np.array(
        [
            1.0 / 15.0,
            0.378474956297847,
            0.5548583770354862,
            0.5548583770354862,
            0.378474956297847,
            1.0 / 15.0,
        ]
    )
    legendre = (63.0 * gll_points**5 - 70.0 * gll_points**3 + 15.0 * gll_points) / 8.0
    derivative = np.zeros((6, 6))
    for left_node in range(6):
        for right_node in range(6):
            if left_node != right_node:
                derivative[left_node, right_node] = legendre[left_node] / (
                    legendre[right_node] * (gll_points[left_node] - gll_points[right_node])
                )
    derivative[0, 0] = -7.5
    derivative[5, 5] = 7.5
    mass_weights = (
        gll_weights[:, None, None] * gll_weights[None, :, None] * gll_weights[None, None, :]
    )
    return (jnp.asarray(derivative, jnp.float32), jnp.asarray(mass_weights[..., None], jnp.float32))


def derive_along(values_in, dimension, matrix):
    einsum_forms = ("ai,...ijke->...ajke", "aj,...ijke->...iake", "ak,...ijke->...ijae")
    return jnp.einsum(einsum_forms[dimension], matrix, values_in, precision=PRECISE)


def derive_back(values_in, dimension, matrix):
    einsum_forms = ("ai,...ajke->...ijke", "aj,...iake->...ijke", "ak,...ijae->...ijke")
    return jnp.einsum(einsum_forms[dimension], matrix, values_in, precision=PRECISE)


def fold_edges(padded, dimension):
    length = padded.shape[dimension]
    interior = lax.slice_in_dim(padded, 1, length - 1, axis=dimension)
    lower_rim = lax.slice_in_dim(padded, 0, 1, axis=dimension)
    upper_rim = lax.slice_in_dim(padded, length - 1, length, axis=dimension)
    middle_shape = list(interior.shape)
    middle_shape[dimension] = length - 4
    middle = jnp.zeros(middle_shape, padded.dtype)
    return interior + jnp.concatenate([lower_rim, middle, upper_rim], axis=dimension)


def fold_pair(values, axis):
    count = values.shape[axis]
    merged = tuple(values.shape[:axis]) + (5 * count,) + tuple(values.shape[axis + 2 :])
    lower = lax.slice_in_dim(values, 0, 5, axis=axis + 1).reshape(merged)
    top = lax.slice_in_dim(values, 5, 6, axis=axis + 1)
    filler_shape = list(top.shape)
    filler_shape[axis + 1] = 4
    top_block = jnp.concatenate(
        [jnp.zeros(filler_shape, values.dtype), top], axis=axis + 1
    ).reshape(merged)
    rim_shape = list(merged)
    rim_shape[axis] = 1
    rim_zeros = jnp.zeros(rim_shape, values.dtype)
    return jnp.concatenate([lower, rim_zeros], axis=axis) + jnp.concatenate(
        [rim_zeros, top_block], axis=axis
    )


def spread_pair(values, axis):
    count = (values.shape[axis] - 1) // 5
    split_shape = tuple(values.shape[:axis]) + (count, 5) + tuple(values.shape[axis + 1 :])
    first = lax.slice_in_dim(values, 0, 5 * count, axis=axis).reshape(split_shape)
    later = lax.slice_in_dim(values, 5, 5 * count + 1, stride=5, axis=axis)
    later = jnp.expand_dims(later, axis + 1)
    return jnp.concatenate([first, later], axis=axis + 1)


def to_grid(local_values):
    blocked = local_values.reshape(6, 6, 6, ELX, ELY, ELZ).transpose(3, 0, 4, 1, 5, 2)
    return fold_pair(fold_pair(fold_pair(blocked, 0), 1), 2)


def to_elements(node_grid):
    blocked = spread_pair(spread_pair(spread_pair(node_grid, 2), 1), 0)
    return blocked.transpose(1, 3, 5, 0, 2, 4).reshape(6, 6, 6, ELX * ELY * ELZ)


def edge_count(extent, place, blocks):
    positions = jnp.arange(extent)
    lower_share = ((positions == 0) & (place > 0)).astype(jnp.float32)
    upper_share = ((positions == extent - 1) & (place < blocks - 1)).astype(jnp.float32)
    return 1.0 + lower_share + upper_share


def edge_table(extent):
    positions = jnp.arange(extent)
    lower_side = (positions == 0).astype(jnp.float32)
    upper_side = (positions == extent - 1).astype(jnp.float32)
    return jnp.stack([lower_side, jnp.ones((extent,), jnp.float32), upper_side], axis=1)


def shards(velocity, base_flow, viscosity, cell_order, coarse_inv):
    derivative, mass_weights = gll_tables()
    elements = velocity.shape[2]
    nodes_x = 5 * ELX + 1
    nodes_y = 5 * ELY + 1
    nodes_z = 5 * ELZ + 1
    grid_shape = (nodes_x, nodes_y, nodes_z)
    cell_ids = cell_order[0]
    slot_of_cell = (
        jnp.zeros((elements,), jnp.int32).at[cell_ids].set(jnp.arange(elements, dtype=jnp.int32))
    )
    dom_index = lax.axis_index("dom")
    sub_index = lax.axis_index("sub")
    dom_count = lax.axis_size("dom")
    sub_count = lax.axis_size("sub")
    share_x = edge_count(nodes_x, dom_index, dom_count)
    share_y = edge_count(nodes_y, sub_index, sub_count)
    inverse_share = (1.0 / (share_x[:, None] * share_y[None, :]))[:, :, None]

    def share_sum(stacked_grid):
        padded = extended(stacked_grid, (("dom", 1), ("sub", 2)), 1)
        summed = fold_edges(fold_edges(padded, 1), 2)
        return summed

    def assemble(local_values):
        return share_sum(to_grid(local_values)[None])[0]

    moving = jnp.take(velocity, slot_of_cell, axis=2).reshape(3, 6, 6, 6, elements)
    base_nodes = jnp.take(base_flow, slot_of_cell, axis=2).reshape(3, 6, 6, 6, elements)
    advect_parts = []
    for component in range(3):
        accumulated = jnp.zeros((6, 6, 6, elements), jnp.float32)
        for dimension in range(3):
            accumulated = accumulated + base_nodes[dimension] * derive_along(
                moving[component], dimension, derivative
            )
            accumulated = accumulated + moving[dimension] * derive_along(
                base_nodes[component], dimension, derivative
            )
        advect_parts.append(-accumulated)
    advect = jnp.stack(advect_parts)
    divergence = (
        derive_along(advect[0], 0, derivative)
        + derive_along(advect[1], 1, derivative)
        + derive_along(advect[2], 2, derivative)
    )
    weighted = mass_weights * jnp.take(viscosity, slot_of_cell, axis=1).reshape(6, 6, 6, elements)
    squared = derivative * derivative
    diag_local = (
        REACTION * mass_weights
        + derive_back(weighted, 0, squared)
        + derive_back(weighted, 1, squared)
        + derive_back(weighted, 2, squared)
    )
    both_grid = share_sum(
        jnp.stack([to_grid(mass_weights * divergence), to_grid(diag_local)], axis=0)
    )
    rhs = both_grid[0]
    inverse_diag = 1.0 / both_grid[1]

    def helmholtz(node_grid):
        local_values = to_elements(node_grid)
        result = REACTION * mass_weights * local_values
        for dimension in range(3):
            result = result + derive_back(
                weighted * derive_along(local_values, dimension, derivative), dimension, derivative
            )
        return assemble(result)

    def precondition(residual):
        coarse_term = jnp.sum(residual * inverse_share)
        coarse_all = lax.all_gather(coarse_term.reshape(1), ("dom", "sub"), axis=0, tiled=True)
        solved = jnp.dot(coarse_inv, coarse_all, precision=PRECISE).reshape(dom_count, sub_count)
        framed = jnp.pad(solved, 1)
        nearby = lax.dynamic_slice(framed, (dom_index, sub_index), (3, 3))
        spread = jnp.dot(
            jnp.dot(edge_table(nodes_x), nearby, precision=PRECISE),
            edge_table(nodes_y).T,
            precision=PRECISE,
        )
        coarse_part = spread[:, :, None] * inverse_share
        return residual * inverse_diag + coarse_part

    def local_inner(left_vec, right_vec):
        return jnp.sum(left_vec * right_vec * inverse_share)

    pressure_grid = jnp.zeros(grid_shape, jnp.float32)
    residual = rhs

    def paired(residual_now, search_now, applied_now):
        return lax.psum(
            (local_inner(residual_now, search_now), local_inner(applied_now, search_now)),
            ("dom", "sub"),
        )

    search = precondition(residual)
    applied = helmholtz(search)
    gamma_now, curvature = paired(residual, search, applied)
    step_size = gamma_now / curvature
    direction = search
    along_dir = applied
    for iteration in range(ITERS):
        pressure_grid = pressure_grid + step_size * direction
        residual = residual - step_size * along_dir
        if iteration + 1 < ITERS:
            search = precondition(residual)
            applied = helmholtz(search)
            gamma_next, curvature = paired(residual, search, applied)
            beta_ratio = gamma_next / gamma_now
            step_size = gamma_next / (curvature - beta_ratio * gamma_next / step_size)
            direction = search + beta_ratio * direction
            along_dir = applied + beta_ratio * along_dir
            gamma_now = gamma_next
    pressure = to_elements(pressure_grid)
    gradient = jnp.stack([derive_along(pressure, dimension, derivative) for dimension in range(3)])
    linear_cells = (advect - gradient).reshape(3, 216, elements)
    linearized = jnp.take(linear_cells, cell_ids, axis=2)
    pressure_slots = jnp.take(pressure.reshape(216, elements), cell_ids, axis=1)
    return (linearized, pressure_slots)


def solution(mesh):
    placed = (
        P(None, None, ("dom", "sub")),
        P(None, None, ("dom", "sub")),
        P(None, ("dom", "sub")),
        P(("dom", "sub"), None),
        P(),
    )
    return jax.shard_map(
        shards,
        mesh=mesh,
        in_specs=placed,
        out_specs=(P(None, None, ("dom", "sub")), P(None, ("dom", "sub"))),
        check_vma=False,
    )
```

profile of v0, /device:TPU:1, one launch (start us, length us, event | category | flops | bytes accessed | tf_op | source)
XLA Modules:
  0.0 658.0 jit_solution(14237363809982286241)
XLA Ops:
  32.7 3.1 reshape.326
  38.5 3.1 reshape.334
  41.9 4.4 collective-permute-start
  47.7 3.4 collective-permute-done.1
  51.2 4.9 collective-permute-start.2
  58.2 3.0 collective-permute-done.3
  63.1 89.9 %all-reduce.48 = f32[256]{0:T(256)S(1)} all-reduce(f32[256]{0:T(256)S(1)} %dynamic-update-slice), channel_id=1, replica_groups=mesh['dom'=32,'sub'=8] {'dom','sub'}, use_global_device_ids=true, to_apply=%add.48 | all-reduce | flops 256 | bytes 2048
  167.6 3.1 reshape.347
  173.6 3.2 collective-permute-done.5
  176.8 4.3 collective-permute-start.6
  183.0 3.1 collective-permute-done.7
  187.1 77.4 %all-reduce.53 = (f32[]{:T(128)}, f32[]{:T(128)}) all-reduce(f32[]{:T(128)} %get-tuple-element.17, f32[]{:T(128)} %get-tuple-element.16), channel_id=1, replica_groups=mesh['dom'=32,'sub'=8] {'dom','sub'}, use_global_device_ids=true, to_apply=%region_3.6 | all-reduce | flops 2 | bytes 16 | tf_op jit(solution)/shard_map/psum | solution.py:233
  267.2 72.7 %all-reduce.49 = f32[256]{0:T(256)S(1)} all-reduce(f32[256]{0:T(256)S(1)} %dynamic-update-slice.1), channel_id=1, replica_groups=mesh['dom'=32,'sub'=8] {'dom','sub'}, use_global_device_ids=true, to_apply=%add.49 | all-reduce | flops 256 | bytes 2048
  355.1 3.2 reshape.360
  358.5 3.7 collective-permute-start.8
  363.5 3.2 collective-permute-done.9
  366.7 4.5 collective-permute-start.10
  377.2 74.9 %all-reduce.52 = (f32[]{:T(128)}, f32[]{:T(128)}) all-reduce(f32[]{:T(128)} %get-tuple-element.15, f32[]{:T(128)} %get-tuple-element.14), channel_id=1, replica_groups=mesh['dom'=32,'sub'=8] {'dom','sub'}, use_global_device_ids=true, to_apply=%region_8.11 | all-reduce | flops 2 | bytes 16 | tf_op jit(solution)/shard_map/psum | solution.py:233
  458.1 72.8 %all-reduce.50 = f32[256]{0:T(256)S(1)} all-reduce(f32[256]{0:T(256)S(1)} %dynamic-update-slice.2), channel_id=1, replica_groups=mesh['dom'=32,'sub'=8] {'dom','sub'}, use_global_device_ids=true, to_apply=%add.50 | all-reduce | flops 256 | bytes 2048
  545.5 3.2 reshape.373
  548.8 3.9 collective-permute-start.12
  554.0 3.2 collective-permute-done.13
  557.2 4.2 collective-permute-start.14
  567.4 75.1 %all-reduce.51 = (f32[]{:T(128)}, f32[]{:T(128)}) all-reduce(f32[]{:T(128)} %get-tuple-element.13, f32[]{:T(128)} %get-tuple-element.12), channel_id=1, replica_groups=mesh['dom'=32,'sub'=8] {'dom','sub'}, use_global_device_ids=true, to_apply=%region_13.16 | all-reduce | flops 2 | bytes 16 | tf_op jit(solution)/shard_map/psum | solution.py:233
  (430 shorter events, 117.5 us)
Async XLA Ops:
  41.9 5.8 collective-permute-start
  46.3 4.8 collective-permute-start.1
  51.2 7.1 %collective-permute-start.2 = (f32[2,13,1,161]{3,2,1,0:T(1,128)S(1)}, f32[2,13,1,161]{3,2,1,0:T(1,128)S(1)}, u32[]{:S(2)}, u32[]{:S(2)}) collective-permute-start(f32[2,13,1,161]{3,2,1,0:T(1,128)S(1)} %get-tuple-element.34), channel_id=1, source_target_pairs={{0,1},{1,2},{2,3},{3,4},{4,5},{5,6},{6,7},{8,9},{9,10},{10,11},{11... | collective-permute-start | bytes 50240 | tf_op jit(solution)/shard_map/ppermute | solution.py:25
  56.1 5.2 collective-permute-start.3
  170.7 169.6 %copy-start.52 = (f32[11,1]{0,1:T(1,128)S(1)}, f32[11,1]{0,1:T(1,128)}, u32[]{:S(2)}) copy-start(f32[11,1]{0,1:T(1,128)} %copy-done.51) | copy-start | bytes 136
  170.7 169.9 %copy-start.38 = (f32[11]{0:T(128)S(1)}, f32[11]{0:T(128)}, u32[]{:S(2)}) copy-start(f32[11]{0:T(128)} %copy-done.37) | copy-start | bytes 136
  170.7 169.9 %copy-start.41 = (f32[11]{0:T(128)S(1)}, f32[11]{0:T(128)}, u32[]{:S(2)}) copy-start(f32[11]{0:T(128)} %copy-done.40) | copy-start | bytes 136
  170.9 2.7 collective-permute-start.4
  172.3 4.5 collective-permute-start.5
  176.8 6.2 collective-permute-start.6
  181.1 5.0 collective-permute-start.7
  358.3 173.1 %copy-start.47 = (f32[3]{0:T(128)S(1)}, f32[3]{0:T(128)}, u32[]{:S(2)}) copy-start(f32[3]{0:T(128)} %copy-done.45) | copy-start | bytes 40
  358.3 173.1 %copy-start.50 = (f32[11,1]{0,1:T(1,128)S(1)}, f32[11,1]{0,1:T(1,128)}, u32[]{:S(2)}) copy-start(f32[11,1]{0,1:T(1,128)} %copy-done.48) | copy-start | bytes 136
  358.3 173.1 %copy-start.53 = (f32[11,1]{0,1:T(1,128)S(1)}, f32[11,1]{0,1:T(1,128)}, u32[]{:S(2)}) copy-start(f32[11,1]{0,1:T(1,128)} %copy-done.51) | copy-start | bytes 136
  358.3 173.4 %copy-start.39 = (f32[11]{0:T(128)S(1)}, f32[11]{0:T(128)}, u32[]{:S(2)}) copy-start(f32[11]{0:T(128)} %copy-done.37) | copy-start | bytes 136
  358.3 173.4 %copy-start.42 = (f32[11]{0:T(128)S(1)}, f32[11]{0:T(128)}, u32[]{:S(2)}) copy-start(f32[11]{0:T(128)} %copy-done.40) | copy-start | bytes 136
  358.5 5.0 collective-permute-start.8
  362.2 4.5 collective-permute-start.9
  366.7 7.0 %collective-permute-start.10 = (f32[1,13,1,161]{3,2,1,0:T(1,128)S(1)}, f32[1,13,1,161]{3,2,1,0:T(1,128)S(1)}, u32[]{:S(2)}, u32[]{:S(2)}) collective-permute-start(f32[1,13,1,161]{3,2,1,0:T(1,128)S(1)} %get-tuple-element.42), channel_id=1, source_target_pairs={{0,1},{1,2},{2,3},{3,4},{4,5},{5,6},{6,7},{8,9},{9,10},{10,11},{11... | collective-permute-start | bytes 25124 | tf_op jit(solution)/shard_map/ppermute | solution.py:25
  371.2 5.0 collective-permute-start.11
  548.8 5.2 collective-permute-start.12
  552.7 4.5 collective-permute-start.13
  557.2 8.0 %collective-permute-start.14 = (f32[1,13,1,161]{3,2,1,0:T(1,128)S(1)}, f32[1,13,1,161]{3,2,1,0:T(1,128)S(1)}, u32[]{:S(2)}, u32[]{:S(2)}) collective-permute-start(f32[1,13,1,161]{3,2,1,0:T(1,128)S(1)} %get-tuple-element.40), channel_id=1, source_target_pairs={{0,1},{1,2},{2,3},{3,4},{4,5},{5,6},{6,7},{8,9},{9,10},{10,11},{11... | collective-permute-start | bytes 25124 | tf_op jit(solution)/shard_map/ppermute | solution.py:25
  561.4 5.0 collective-permute-start.15
  (46 other events, 2355.5 us)
where the time goes:
time: 664 us; the launch traced here: 658 us
  blocking collectives  463 us (70%)
  local copies, waits for them, and re-layouts  80.1 us (12%)
  starting transfers between devices  44.1 us (7%)
  waiting for transfers between devices  22.8 us (3%)
  matrix products  19.2 us (3%)
  other arithmetic  15.9 us (2%)
  between operations  13.1 us (2%)
    unnamed x3, blocking collectives  235 us
    psum x3, blocking collectives, paired(): lax.psum((local_inner(residual_now, search_now), local_inner(applied_now,...  227 us
    ppermute x8, starting transfers between devices, extended(): lax.ppermute(tail, axis, [(i, (i + 1) % count) for i in range(ends)])  31.3 us
    ppermute x8, waiting for transfers between devices, extended(): lax.ppermute(head, axis, [((i + 1) % count, i) for i in range(ends)])  22.8 us
    reshape x5, local copies, waits for them, and re-layouts, fold_pair(): top_block = jnp.concatenate([jnp.zeros(filler_shape, values.dtype), top],...  15.8 us
  transfers between devices with their start and end apart: 16, of which 8 were waited for; matrix products, arithmetic and copies ran while one was open for 0% of the time, Pallas kernels for 0%

commit v1 on v0

v1 whole, which is shorter than its diff:
```python
import functools

import jax
import jax.numpy as jnp
import ml_dtypes
import numpy as np
from jax import lax
from jax.experimental import pallas as pl
from jax.experimental.pallas import tpu as pltpu
from jax.sharding import PartitionSpec as P

F32 = jnp.float32
BF16 = jnp.bfloat16
MESH = pl.DeviceIdType.MESH
REACTION = 0.001
DOM = 32
SUB = 8
ROWS = 224
NAT = 216
NFACE = 9


def gll_tables():
    points = np.array(
        [
            -1.0,
            -0.7650553239294647,
            -0.2852315164806451,
            0.2852315164806451,
            0.7650553239294647,
            1.0,
        ]
    )
    weights = np.array(
        [
            1.0 / 15.0,
            0.378474956297847,
            0.5548583770354862,
            0.5548583770354862,
            0.378474956297847,
            1.0 / 15.0,
        ]
    )
    legendre = (63.0 * points**5 - 70.0 * points**3 + 15.0 * points) / 8.0
    derivative = np.zeros((6, 6))
    for a in range(6):
        for b in range(6):
            if a != b:
                derivative[a, b] = legendre[a] / (legendre[b] * (points[a] - points[b]))
    derivative[0, 0] = -7.5
    derivative[5, 5] = 7.5
    mass = weights[:, None, None] * weights[None, :, None] * weights[None, None, :]
    return (
        derivative.astype(np.float32).astype(np.float64),
        mass.astype(np.float32).astype(np.float64).reshape(-1),
    )


def class_rows():
    mid = (1, 2, 3, 4)
    rows = [(i, j, k) for i in mid for j in mid for k in mid]
    for i in (0, 5):
        rows += [(i, j, k) for j in mid for k in mid]
        rows += [(i, j, k) for k in (0, 5) for j in mid]
        rows += [(i, j, k) for j in (0, 5) for k in mid]
        for j in (0, 5):
            for k in (0, 5):
                rows += [(i, j, k), None]
    for j in (0, 5):
        rows += [(i, j, k) for i in mid for k in mid]
        rows += [(i, j, k) for k in (0, 5) for i in mid]
    for k in (0, 5):
        rows += [(i, j, k) for i in mid for j in mid]
    return rows


def split_np(matrix):
    single = matrix.astype(np.float32)
    high = single.astype(ml_dtypes.bfloat16)
    low = (single - high.astype(np.float32)).astype(ml_dtypes.bfloat16)
    return high, low


def tables():
    derivative, mass = gll_tables()
    eye = np.eye(6)
    parts = [
        np.kron(np.kron(derivative, eye), eye),
        np.kron(np.kron(eye, derivative), eye),
        np.kron(np.kron(eye, eye), derivative),
    ]
    rows = class_rows()
    assert len(rows) == ROWS
    pick = np.zeros((ROWS, NAT))
    for at, node in enumerate(rows):
        if node is not None:
            pick[at, 36 * node[0] + 6 * node[1] + node[2]] = 1.0
    natural = np.zeros((3, ROWS, 256))
    from_class = np.zeros((3, ROWS, 256))
    back = np.zeros((ROWS, 768))
    divergence = np.zeros((ROWS, 768))
    squares = np.zeros((ROWS, 256))
    mass_class = pick @ mass
    for m in range(3):
        natural[m, :NAT, :NAT] = parts[m]
        from_class[m, :NAT, :ROWS] = parts[m] @ pick.T
        back[:, ROWS * m : ROWS * m + NAT] = pick @ parts[m].T
        divergence[:, ROWS * m : ROWS * m + NAT] = mass_class[:, None] * (pick @ parts[m])
        squares[:, :NAT] += pick @ (parts[m].astype(np.float32) ** 2).T
    to_natural = np.zeros((ROWS, 256))
    to_natural[:NAT, :ROWS] = pick.T
    mass_natural = np.zeros((ROWS,))
    mass_natural[:NAT] = mass
    pad = (pick.sum(1) == 0).astype(np.float32)
    out = []
    for matrix in (
        natural.reshape(3 * ROWS, 256),
        from_class.reshape(3 * ROWS, 256),
        back,
        divergence,
        squares,
    ):
        out += list(split_np(matrix))
    out.append(to_natural.astype(ml_dtypes.bfloat16))
    wide = lambda v: np.broadcast_to(v[:, None], (ROWS, 128)).astype(np.float32)
    out += [wide(mass_natural), wide(REACTION * mass_class), wide(pad)]
    lane = np.arange(128)[None, :] * np.ones((8, 1), int)
    sub = np.arange(8)[:, None] * np.ones((1, 128), int)
    ex, ey, ez = lane // 64, (lane // 32) % 2, lane % 32
    upper = sub >= 4
    corner_high = (sub % 4) == 2
    corner_low = (sub % 4) == 0
    masks = np.stack(
        [
            ex == 0,
            ex == 1,
            ey == 0,
            ey == 1,
            upper & (ey == 0),
            ~upper & (ey == 1),
            ez < 31,
            ez > 0,
            upper & (ez < 31),
            ~upper & (ez > 0),
            corner_high & (ez < 31),
            corner_low & (ez > 0),
            upper & (ey == 1),
            ~upper & (ey == 0),
            upper & (ey == 1) & (ex == 1),
            ~upper & (ey == 0) & (ex == 1),
            upper & (ey == 1) & (ex == 0),
            ~upper & (ey == 0) & (ex == 0),
        ]
    ).astype(np.float32)
    out.append(masks)
    side_x = [1, 0, 2, 0, 2, 1, 1]
    low_x = np.stack([(s == 0) & (ex == 0) for s in side_x])
    high_x = np.stack([(s == 2) & (ex == 1) for s in side_x])
    none = np.zeros((8, 128), bool)
    low_y = np.stack([none, none, none, ~upper & (ey == 0), ~upper & (ey == 0), ey == 0, none])
    high_y = np.stack([none, none, none, upper & (ey == 1), upper & (ey == 1), none, ey == 1])
    out.append(np.stack([low_x, high_x, low_y, high_y]).astype(np.float32))
    column = np.arange(256)
    place = np.zeros((3, DOM, 256))
    spread = np.zeros((3, 256, 128))
    lanes = np.arange(128)
    for fx in range(3):
        for dom in range(DOM):
            place[fx, dom] = (column // 8) == dom + fx - 1
        f = lanes % 16
        spread[fx] = (
            ((f // 3) == fx)[None, :]
            & (f < 9)[None, :]
            & ((column % 8)[:, None] == (lanes // 16 + f % 3 - 1)[None, :])
        )
    out.append(place.astype(np.float32))
    out.append(spread.reshape(768, 128).astype(ml_dtypes.bfloat16))
    return out


def dot(a, b):
    return jnp.dot(a, b, preferred_element_type=F32)


def halves(x):
    high = x.astype(BF16)
    low = (x - high.astype(F32)).astype(BF16)
    return high, low


def thirds(x):
    high = x.astype(BF16)
    rest = x - high.astype(F32)
    mid = rest.astype(BF16)
    low = (rest - mid.astype(F32)).astype(BF16)
    return high, mid, low


def product(high_ref, low_ref, x):
    depth = high_ref.shape[1]
    if x.shape[0] < depth:
        x = jnp.concatenate([x, jnp.zeros((depth - x.shape[0], x.shape[1]), F32)], axis=0)
    width = x.shape[1]
    high, low = halves(x)
    both = dot(high_ref[...], jnp.concatenate([high, low], axis=1))
    return both[:, :width] + both[:, width:] + dot(low_ref[...], high)


def pad_rows(x, rows):
    return jnp.concatenate([x, jnp.zeros((rows - x.shape[0], x.shape[1]), F32)], axis=0)


def move_lanes(x, select, transposed):
    rows = x.shape[0]
    stacked = jnp.concatenate(thirds(x), axis=0)
    if transposed:
        moved = lax.dot_general(
            stacked, select, (((1,), (1,)), ((), ())), preferred_element_type=F32
        )
    else:
        moved = dot(stacked, select)
    return moved[:rows] + moved[rows : 2 * rows] + moved[2 * rows :]


def roll(x, shift, axis):
    return pltpu.roll(x, shift, axis)


def cube(x):
    return x.reshape(x.shape[0] // 8, 8, 128)


def flat(x):
    return x.reshape(x.shape[0] * 8, 128)


def swap(x):
    return roll(x, 4, 1)


def block_sum(t, mask):
    inner, a0, a5, b0, b5, z0, z5 = (
        t[0:8],
        t[8:13],
        t[13:18],
        t[18:21],
        t[21:24],
        t[24:26],
        t[26:28],
    )
    a0, a5 = a0 + mask(1) * roll(a5, 64, 2), a5 + mask(0) * roll(a0, 64, 2)
    b0, b5 = b0 + mask(3) * roll(b5, 32, 2), b5 + mask(2) * roll(b0, 96, 2)
    edge = jnp.concatenate([a0[3:5], a5[3:5]], axis=0)
    turned = swap(edge)
    edge = edge + mask(4) * roll(turned, 96, 2) + mask(5) * roll(turned, 32, 2)
    z0, z5 = z0 + mask(7) * roll(z5, 1, 2), z5 + mask(6) * roll(z0, 127, 2)
    rim = jnp.concatenate([a0[2:3], a5[2:3], b0[2:3], b5[2:3]], axis=0)
    turned = swap(rim)
    rim = rim + mask(8) * roll(turned, 127, 2) + mask(9) * roll(turned, 1, 2)
    corner = jnp.concatenate([edge[1:2], edge[3:4]], axis=0)
    corner = (
        corner
        + mask(10) * roll(roll(corner, 2, 1), 127, 2)
        + mask(11) * roll(roll(corner, 6, 1), 1, 2)
    )
    return jnp.concatenate(
        [
            inner,
            a0[0:2],
            rim[0:1],
            edge[0:1],
            corner[0:1],
            a5[0:2],
            rim[1:2],
            edge[2:3],
            corner[1:2],
            b0[0:2],
            rim[2:3],
            b5[0:2],
            rim[3:4],
            z0,
            z5,
        ],
        axis=0,
    )


def add_neighbours(t, got, mask, has):
    left, right, down, up = has
    from_right, from_left, from_up, from_down, corners = got
    a0, a5, b0, b5 = t[8:13], t[13:18], t[18:21], t[21:24]
    a5 = a5 + (right * mask(1)) * roll(from_right, 64, 2)
    a0 = a0 + (left * mask(0)) * roll(from_left, 64, 2)
    b5 = b5 + (up * mask(3)) * roll(from_up[0:3], 32, 2)
    b0 = b0 + (down * mask(2)) * roll(from_down[0:3], 96, 2)
    up_rows = (up * mask(12)) * roll(swap(from_up[3:7]), 32, 2)
    down_rows = (down * mask(13)) * roll(swap(from_down[3:7]), 96, 2)
    edge = up_rows + down_rows
    e0 = a0[3:5] + edge[0:2]
    e5 = a5[3:5] + edge[2:4]
    e5 = e5 + (right * up * mask(14)) * roll(swap(corners[0]), 96, 2)
    e5 = e5 + (right * down * mask(15)) * roll(swap(corners[1]), 32, 2)
    e0 = e0 + (left * up * mask(16)) * roll(swap(corners[2]), 96, 2)
    e0 = e0 + (left * down * mask(17)) * roll(swap(corners[3]), 32, 2)
    return jnp.concatenate([t[0:8], a0[0:3], e0, a5[0:3], e5, b0, b5, t[24:28]], axis=0)


def by_kind(t):
    total = lambda *spans: sum(jnp.sum(t[a:b], axis=0, keepdims=True) for a, b in spans)
    return jnp.concatenate(
        [
            total((0, 8), (24, 28)),
            total((8, 11)),
            total((13, 16)),
            total((11, 13)),
            total((16, 18)),
            total((18, 21)),
            total((21, 24)),
        ],
        axis=0,
    )


def from_kinds(v):
    order = [0] * 8 + [1] * 3 + [3] * 2 + [2] * 3 + [4] * 2 + [5] * 3 + [6] * 3 + [0] * 4
    return jnp.concatenate([v[k : k + 1] for k in order], axis=0)


def total_of(x):
    return jnp.sum(jnp.sum(x, axis=0, keepdims=True), axis=2, keepdims=True)


def kernel(
    vel_ref,
    base_ref,
    visc_ref,
    order_ref,
    coarse_ref,
    nat_hi,
    nat_lo,
    cls_hi,
    cls_lo,
    back_hi,
    back_lo,
    div_hi,
    div_lo,
    sq_hi,
    sq_lo,
    out_pick,
    mass_ref,
    react_ref,
    pad_ref,
    mask_ref,
    side_ref,
    place_ref,
    spread_ref,
    lin_ref,
    press_ref,
    field,
    y_up,
    y_down,
    got_x,
    got_y,
    got_c,
    row_a,
    row_b,
    all_a,
    all_b,
    weight_ref,
    solve_ref,
    send_h,
    recv_h,
    send_a,
    recv_a,
    send_b,
    recv_b,
):
    dom = lax.axis_index("dom")
    sub = lax.axis_index("sub")
    dom_next, dom_prev = lax.rem(dom + 1, DOM), lax.rem(dom + DOM - 1, DOM)
    sub_next, sub_prev = lax.rem(sub + 1, SUB), lax.rem(sub + SUB - 1, SUB)
    barrier = pltpu.get_barrier_semaphore()

    def greet(where):
        pl.semaphore_signal(barrier, inc=1, device_id=where, device_id_type=MESH)

    for step in range(1, SUB):
        greet((dom, lax.rem(sub + step, SUB)))
    for step in range(1, DOM):
        greet((lax.rem(dom + step, DOM), sub))
    diagonals = (
        (dom_prev, sub_prev),
        (dom_prev, sub_next),
        (dom_next, sub_prev),
        (dom_next, sub_next),
    )
    for where in diagonals:
        greet(where)

    mask = lambda at: mask_ref[at]

    def flag(condition):
        return jnp.where(condition, 1.0, 0.0).astype(F32)

    has = (flag(dom > 0), flag(dom < DOM - 1), flag(sub > 0), flag(sub < SUB - 1))

    vel = [pad_rows(vel_ref[c], ROWS) for c in range(3)]
    base = [pad_rows(base_ref[c], ROWS) for c in range(3)]
    advect = []
    for c in range(3):
        grads = product(nat_hi, nat_lo, jnp.concatenate([vel[c], base[c]], axis=1))
        acc = jnp.zeros((ROWS, 128), F32)
        for m in range(3):
            part = grads[ROWS * m : ROWS * (m + 1)]
            acc = acc - base[m] * part[:, :128] - vel[m] * part[:, 128:]
        advect.append(acc)
        lin_ref[c] = acc[:NAT]
    select = jnp.where(
        lax.broadcasted_iota(jnp.int32, (128, 128), 0) == order_ref[...], 1.0, 0.0
    ).astype(BF16)
    moved = move_lanes(
        jnp.concatenate(
            [
                product(div_hi, div_lo, jnp.concatenate(advect, axis=0)),
                pad_rows(visc_ref[...], ROWS),
            ],
            axis=0,
        ),
        select,
        True,
    )
    rhs_own = cube(moved[:ROWS])
    weighted = mass_ref[...] * moved[ROWS:]
    weight_ref[...] = jnp.concatenate([weighted, weighted, weighted], axis=0)
    diag_own = cube(react_ref[...] + product(sq_hi, sq_lo, weighted))

    left, right, down, up = has
    side_l, side_r = (0.5 * left) * side_ref[0], (0.5 * right) * side_ref[1]
    side_d, side_u = (0.5 * down) * side_ref[2], (0.5 * up) * side_ref[3]
    along_x = (side_l, 1.0 - side_l - side_r, side_r)
    along_y = (side_d, 1.0 - side_d - side_u, side_u)

    def coarse_parts(kinds):
        return [
            jnp.sum(along_x[fx] * along_y[fy] * kinds, axis=0, keepdims=True)
            for fx in range(3)
            for fy in range(3)
        ]

    def spread_coarse(solved):
        values = 0.0
        for fx in range(3):
            inner = sum(solved[3 * fx + fy] * along_y[fy] for fy in range(3))
            values = values + along_x[fx] * inner
        return from_kinds(values)

    lane = lax.broadcasted_iota(jnp.int32, (16, 128), 1)
    slot = lax.broadcasted_iota(jnp.int32, (16, 128), 0)
    home = lane == 16 * sub + slot

    def send(src, dst, send_sem, recv_sem, where):
        pltpu.make_async_remote_copy(
            src_ref=src,
            dst_ref=dst,
            send_sem=send_sem,
            recv_sem=recv_sem,
            device_id=where,
            device_id_type=MESH,
        ).start()

    def wait_for(ref, sem):
        pltpu.make_async_copy(ref, ref, sem).wait()

    def start_gather(at, partials):
        count = len(partials)
        stack = jnp.concatenate(partials, axis=0)
        sums = jnp.sum(jnp.sum(stack, axis=1), axis=1, keepdims=True)
        if count < 16:
            sums = jnp.concatenate([sums, jnp.zeros((16 - count, 1), F32)], axis=0)
        row = jnp.sum(jnp.where(home, sums, 0.0), axis=0, keepdims=True)
        row_a[at] = row
        for step in range(1, SUB):
            send(
                row_a.at[at],
                all_a.at[at, step - 1],
                send_a.at[at],
                recv_a.at[at],
                (dom, lax.rem(sub + step, SUB)),
            )
        return row

    def forward_gather(at, row):
        wait_for(all_a.at[at], recv_a.at[at])
        row = row + jnp.sum(all_a[at], axis=0)
        row_b[at] = row
        for step in range(1, DOM):
            send(
                row_b.at[at],
                all_b.at[at, dom],
                send_b.at[at],
                recv_b.at[at],
                (lax.rem(dom + step, DOM), sub),
            )
        all_b[at, dom] = row

    def finish_gather(at):
        wait_for(all_b.at[at, 0 : DOM - 1], recv_b.at[at])
        return all_b[at].reshape(DOM, 128)

    def start_halo(at, which, own):
        t = block_sum(own, mask)
        field[at] = t
        y_up[at, 0:3] = t[21:24]
        y_up[at, 3:5] = t[11:13]
        y_up[at, 5:7] = t[16:18]
        y_down[at, 0:3] = t[18:21]
        y_down[at, 3:5] = t[11:13]
        y_down[at, 5:7] = t[16:18]
        ss, rs = send_h.at[which], recv_h.at[which]
        send(field.at[at, 8:13], got_x.at[at, 0], ss.at[0], rs.at[0], (dom_prev, sub))
        send(field.at[at, 13:18], got_x.at[at, 1], ss.at[0], rs.at[0], (dom_next, sub))
        send(y_down.at[at], got_y.at[at, 0], ss.at[1], rs.at[1], (dom, sub_prev))
        send(y_up.at[at], got_y.at[at, 1], ss.at[1], rs.at[1], (dom, sub_next))
        for n, where in enumerate(diagonals):
            src = field.at[at, 11:13] if n < 2 else field.at[at, 16:18]
            send(src, got_c.at[at, n], ss.at[2], rs.at[2], where)
        return t

    def finish_halo(at, which, t):
        rs = recv_h.at[which]
        wait_for(got_x.at[at], rs.at[0])
        wait_for(got_y.at[at], rs.at[1])
        wait_for(got_c.at[at], rs.at[2])
        got = (
            got_x[at, 0],
            got_x[at, 1],
            got_y[at, 0],
            got_y[at, 1],
            [got_c[at, n] for n in range(4)],
        )
        return add_neighbours(t, got, mask, has)

    def apply(u):
        v = flat(u)
        g = product(cls_hi, cls_lo, v)
        h = pad_rows(g * weight_ref[...], 768)
        return cube(product(back_hi, back_lo, h) + react_ref[...] * v)

    def inner(a, b):
        return jnp.sum(a * b, axis=0, keepdims=True)

    def results(everyone, dots):
        rows = cube(everyone)
        terms = [
            jnp.sum(rows * cube(solve_ref[a]), axis=0, keepdims=True) for a in range(NFACE)
        ]
        column = jnp.sum(rows, axis=0, keepdims=True)
        which = lax.broadcasted_iota(jnp.int32, (1, 8, 128), 2) % 16
        terms += [jnp.where(which == NFACE + d, column, 0.0) for d in range(dots)]
        sums = jnp.sum(
            jnp.sum(jnp.concatenate(terms, axis=0), axis=1, keepdims=True), axis=2, keepdims=True
        )
        return [sums[n] for n in range(NFACE + dots)]

    pl.semaphore_wait(barrier, SUB - 1 + DOM - 1 + 4)
    row = start_gather(0, coarse_parts(by_kind(rhs_own)))
    rhs_block = start_halo(0, 0, rhs_own)
    diag_block = start_halo(1, 1, diag_own)

    chosen = []
    for ax in (-1, 0, 1):
        for ay in (-1, 0, 1):
            at = jnp.clip((dom + ax) * SUB + sub + ay, 0, DOM * SUB - 1)
            chosen.append(coarse_ref[pl.ds(at, 1), :])
    for a in range(NFACE):
        wide = jnp.concatenate([place_ref[fx] * chosen[a] for fx in range(3)], axis=1)
        pieces = thirds(wide)
        solve_ref[a] = sum(dot(piece, spread_ref[...]) for piece in pieces)

    forward_gather(0, row)
    r_all = finish_halo(0, 0, rhs_block)
    d_all = finish_halo(1, 1, diag_block)
    inverse = 1.0 / (d_all + cube(pad_ref[...]))
    solved = results(finish_gather(0), 0)
    r_own = rhs_own
    z = inverse * r_all + spread_coarse(solved)

    direction = None
    for it in range(3):
        w_own = apply(z)
        dots = [inner(z, r_own), inner(z, w_own)]
        last = it == 2
        parts = coarse_parts(by_kind(w_own)) if not last else [jnp.zeros((1, 8, 128), F32)] * 9
        row = start_gather(it + 1, parts + dots)
        if not last:
            w_block = start_halo(it + 2, it + 2, w_own)
        forward_gather(it + 1, row)
        if not last:
            w_all = finish_halo(it + 2, it + 2, w_block)
        got = results(finish_gather(it + 1), 2)
        gamma, curve = got[NFACE], got[NFACE + 1]
        solved_w = got[:NFACE]
        if it == 0:
            alpha = gamma / curve
            direction = z
            q = alpha * direction
            if not last:
                along_own, along_all, along_solved = w_own, w_all, solved_w
        else:
            beta = gamma / gamma_before
            alpha = gamma / (curve - beta * gamma / alpha)
            direction = z + beta * direction
            q = q + alpha * direction
            if not last:
                along_own = w_own + beta * along_own
                along_all = w_all + beta * along_all
                along_solved = [a + beta * b for a, b in zip(solved_w, along_solved)]
        gamma_before = gamma
        if not last:
            r_own = r_own - alpha * along_own
            r_all = r_all - alpha * along_all
            solved = [a - alpha * b for a, b in zip(solved, along_solved)]
            z = inverse * r_all + spread_coarse(solved)

    slots = pad_rows(move_lanes(flat(q), select, False), 256)
    press_ref[...] = sum(dot(out_pick[...], piece) for piece in thirds(slots))[:NAT]
    grads = product(cls_hi, cls_lo, slots)
    for c in range(3):
        lin_ref[c] = lin_ref[c] - grads[ROWS * c : ROWS * c + NAT]

    for at in range(4):
        wait_for(all_a.at[at], send_a.at[at])
        wait_for(all_b.at[at, 0 : DOM - 1], send_b.at[at])
        wait_for(got_x.at[at], send_h.at[at, 0])
        wait_for(got_y.at[at], send_h.at[at, 1])
        wait_for(got_c.at[at], send_h.at[at, 2])


def shards(velocity, base_flow, viscosity, cell_order, coarse_inv):
    args = [velocity, base_flow, viscosity, cell_order, coarse_inv]
    args += [jnp.asarray(t) for t in tables()]
    vmem = pl.BlockSpec(memory_space=pltpu.VMEM)
    dma = pltpu.SemaphoreType.DMA
    return pl.pallas_call(
        kernel,
        out_shape=(
            jax.ShapeDtypeStruct((3, NAT, 128), F32),
            jax.ShapeDtypeStruct((NAT, 128), F32),
        ),
        in_specs=[vmem] * len(args),
        out_specs=(vmem, vmem),
        scratch_shapes=[
            pltpu.VMEM((4, 28, 8, 128), F32),
            pltpu.VMEM((4, 7, 8, 128), F32),
            pltpu.VMEM((4, 7, 8, 128), F32),
            pltpu.VMEM((4, 2, 5, 8, 128), F32),
            pltpu.VMEM((4, 2, 7, 8, 128), F32),
            pltpu.VMEM((4, 4, 2, 8, 128), F32),
            pltpu.VMEM((4, 1, 128), F32),
            pltpu.VMEM((4, 1, 128), F32),
            pltpu.VMEM((4, SUB - 1, 1, 128), F32),
            pltpu.VMEM((4, DOM, 1, 128), F32),
            pltpu.VMEM((3 * ROWS, 128), F32),
            pltpu.VMEM((NFACE, DOM, 128), F32),
            dma((4, 3)),
            dma((4, 3)),
            dma((4,)),
            dma((4,)),
            dma((4,)),
            dma((4,)),
        ],
        compiler_params=pltpu.CompilerParams(
            collective_id=0, has_side_effects=True, vmem_limit_bytes=48 << 20
        ),
    )(*args)


def solution(mesh):
    placed = (
        P(None, None, ("dom", "sub")),
        P(None, None, ("dom", "sub")),
        P(None, ("dom", "sub")),
        P(("dom", "sub"), None),
        P(),
    )
    return jax.shard_map(
        shards,
        mesh=mesh,
        in_specs=placed,
        out_specs=(P(None, None, ("dom", "sub")), P(None, ("dom", "sub"))),
        check_vma=False,
    )
```

time: 664 us -> 74.9 us (0.11)
  blocking collectives: 463 us -> 0 us
  local copies, waits for them, and re-layouts: 80.1 us -> 22.6 us
  Pallas kernels: 0 us -> 50.8 us
  starting transfers between devices: 44.1 us -> 0 us
  waiting for transfers between devices: 22.8 us -> 0 us
  matrix products: 19.2 us -> 0 us
  other arithmetic: 15.9 us -> 0 us
  between operations: 13.1 us -> 0.67 us
    unnamed x3 -> x0, blocking collectives: 235 us -> none
    psum x3 -> x0, blocking collectives: 227 us -> none  [paired(): lax.psum((local_inner(residual_now, search_now), local_inner(applied_now,...]
    pallas_call x0 -> x1, Pallas kernels: none -> 50.8 us  [shards(): pl.pallas_call(kernel, out_shape=(jax.ShapeDtypeStruct((3, NAT, 128), F32...]
    ppermute x16 -> x0, starting transfers between devices: 44.1 us -> none  [the longest x8 31.3 us: extended(): lax.ppermute(tail, axis, [(i, (i + 1) % count) for i in range(ends)])]
    reshape x40 -> x0, local copies, waits for them, and re-layouts: 41.5 us -> none  [the longest x5 15.8 us: fold_pair(): top_block = jnp.concatenate([jnp.zeros(filler_shape, values.dtype), top],...]
    ppermute x16 -> x0, waiting for transfers between devices: 22.8 us -> none  [the longest x8 22.8 us: extended(): lax.ppermute(head, axis, [((i + 1) % count, i) for i in range(ends)])]
    dot_general x54 -> x0, matrix products: 19.2 us -> none  [the longest x33 13.1 us: derive_along(): jnp.einsum(einsum_forms[dimension], matrix, values_in, precision=PRECISE)]
    unnamed x129 -> x48, local copies, waits for them, and re-layouts: 10.6 us -> 22.6 us
  transfers between devices with their start and end apart: 16 -> 0, of which waited for: 8 -> 0; matrix products, arithmetic and copies ran while one was open for 0% -> 0% of each run, Pallas kernels for 0% -> 0%
where the time goes in v1:
time: 74.9 us; the launch traced here: 74.1 us
  Pallas kernels  50.8 us (68%)
  local copies, waits for them, and re-layouts  22.6 us (30%)
    pallas_call x1, Pallas kernels, shards(): pl.pallas_call(kernel, out_shape=(jax.ShapeDtypeStruct((3, NAT, 128), F32...  50.8 us
    unnamed x48, local copies, waits for them, and re-layouts  22.6 us

profile of v1, /device:TPU:1, one launch (start us, length us, event | category | flops | bytes accessed | tf_op | source)
XLA Modules:
  0.0 74.1 jit_solution(1693119015842251797)
XLA Ops:
  0.6 1.0 %copy-done = bf16[224,768]{1,0:T(8,128)(2,1)S(1)} copy-done((bf16[224,768]{1,0:T(8,128)(2,1)S(1)}, bf16[224,768]{1,0:T(8,128)(2,1)}, u32[]{:S(2)}) %copy-start) | copy-done | bytes 344088
  1.6 1.0 %copy-done.1 = bf16[224,768]{1,0:T(8,128)(2,1)S(1)} copy-done((bf16[224,768]{1,0:T(8,128)(2,1)S(1)}, bf16[224,768]{1,0:T(8,128)(2,1)}, u32[]{:S(2)}) %copy-start.1) | copy-done | bytes 344088
  2.6 1.0 %copy-done.2 = bf16[224,768]{1,0:T(8,128)(2,1)S(1)} copy-done((bf16[224,768]{1,0:T(8,128)(2,1)S(1)}, bf16[224,768]{1,0:T(8,128)(2,1)}, u32[]{:S(2)}) %copy-start.2) | copy-done | bytes 344088
  3.6 1.0 %copy-done.3 = bf16[224,768]{1,0:T(8,128)(2,1)S(1)} copy-done((bf16[224,768]{1,0:T(8,128)(2,1)S(1)}, bf16[224,768]{1,0:T(8,128)(2,1)}, u32[]{:S(2)}) %copy-start.3) | copy-done | bytes 344088
  4.6 1.0 %copy-done.4 = bf16[672,256]{1,0:T(8,128)(2,1)S(1)} copy-done((bf16[672,256]{1,0:T(8,128)(2,1)S(1)}, bf16[672,256]{1,0:T(8,128)(2,1)}, u32[]{:S(2)}) %copy-start.4) | copy-done | bytes 344088
  5.5 1.0 %copy-done.5 = bf16[672,256]{1,0:T(8,128)(2,1)S(1)} copy-done((bf16[672,256]{1,0:T(8,128)(2,1)S(1)}, bf16[672,256]{1,0:T(8,128)(2,1)}, u32[]{:S(2)}) %copy-start.5) | copy-done | bytes 344088
  6.5 1.0 %copy-done.6 = bf16[672,256]{1,0:T(8,128)(2,1)S(1)} copy-done((bf16[672,256]{1,0:T(8,128)(2,1)S(1)}, bf16[672,256]{1,0:T(8,128)(2,1)}, u32[]{:S(2)}) %copy-start.6) | copy-done | bytes 344088
  7.5 1.0 %copy-done.7 = bf16[672,256]{1,0:T(8,128)(2,1)S(1)} copy-done((bf16[672,256]{1,0:T(8,128)(2,1)S(1)}, bf16[672,256]{1,0:T(8,128)(2,1)}, u32[]{:S(2)}) %copy-start.7) | copy-done | bytes 344088
  8.5 1.0 %copy-done.8 = f32[3,216,128]{2,1,0:T(8,128)S(1)} copy-done((f32[3,216,128]{2,1,0:T(8,128)S(1)}, f32[3,216,128]{2,1,0:T(8,128)}, u32[]{:S(2)}) %copy-start.8) | copy-done | bytes 331800
  9.4 1.0 %copy-done.9 = f32[3,216,128]{2,1,0:T(8,128)S(1)} copy-done((f32[3,216,128]{2,1,0:T(8,128)S(1)}, f32[3,216,128]{2,1,0:T(8,128)}, u32[]{:S(2)}) %copy-start.9) | copy-done | bytes 331800
  10.4 0.9 %copy-done.10 = f32[256,256]{1,0:T(8,128)S(1)} copy-done((f32[256,256]{1,0:T(8,128)S(1)}, f32[256,256]{1,0:T(8,128)}, u32[]{:S(2)}) %copy-start.10) | copy-done | bytes 262168
  11.4 0.9 %copy-done.11 = bf16[768,128]{1,0:T(8,128)(2,1)S(1)} copy-done((bf16[768,128]{1,0:T(8,128)(2,1)S(1)}, bf16[768,128]{1,0:T(8,128)(2,1)}, u32[]{:S(2)}) %copy-start.11) | copy-done | bytes 196632
  12.3 0.9 %copy-done.12 = f32[4,7,8,128]{3,2,1,0:T(8,128)S(1)} copy-done((f32[4,7,8,128]{3,2,1,0:T(8,128)S(1)}, f32[4,7,8,128]{3,2,1,0:T(8,128)}, u32[]{:S(2)}) %copy-start.12) | copy-done | bytes 114712
  13.2 0.9 %copy-done.13 = f32[224,128]{1,0:T(8,128)S(1)} copy-done((f32[224,128]{1,0:T(8,128)S(1)}, f32[224,128]{1,0:T(8,128)}, u32[]{:S(2)}) %copy-start.13) | copy-done | bytes 114712
  14.1 0.9 %copy-done.14 = f32[224,128]{1,0:T(8,128)S(1)} copy-done((f32[224,128]{1,0:T(8,128)S(1)}, f32[224,128]{1,0:T(8,128)}, u32[]{:S(2)}) %copy-start.14) | copy-done | bytes 114712
  15.0 0.9 %copy-done.15 = f32[224,128]{1,0:T(8,128)S(1)} copy-done((f32[224,128]{1,0:T(8,128)S(1)}, f32[224,128]{1,0:T(8,128)}, u32[]{:S(2)}) %copy-start.15) | copy-done | bytes 114712
  15.9 0.9 %copy-done.16 = bf16[224,256]{1,0:T(8,128)(2,1)S(1)} copy-done((bf16[224,256]{1,0:T(8,128)(2,1)S(1)}, bf16[224,256]{1,0:T(8,128)(2,1)}, u32[]{:S(2)}) %copy-start.16) | copy-done | bytes 114712
  16.8 0.9 %copy-done.17 = bf16[224,256]{1,0:T(8,128)(2,1)S(1)} copy-done((bf16[224,256]{1,0:T(8,128)(2,1)S(1)}, bf16[224,256]{1,0:T(8,128)(2,1)}, u32[]{:S(2)}) %copy-start.17) | copy-done | bytes 114712
  17.7 0.9 %copy-done.18 = bf16[224,256]{1,0:T(8,128)(2,1)S(1)} copy-done((bf16[224,256]{1,0:T(8,128)(2,1)S(1)}, bf16[224,256]{1,0:T(8,128)(2,1)}, u32[]{:S(2)}) %copy-start.18) | copy-done | bytes 114712
  18.6 0.9 %copy-done.19 = f32[216,128]{1,0:T(8,128)S(1)} copy-done((f32[216,128]{1,0:T(8,128)S(1)}, f32[216,128]{1,0:T(8,128)}, u32[]{:S(2)}) %copy-start.19) | copy-done | bytes 110616
  19.5 0.9 %copy-done.20 = f32[3,32,256]{2,1,0:T(8,128)S(1)} copy-done((f32[3,32,256]{2,1,0:T(8,128)S(1)}, f32[3,32,256]{2,1,0:T(8,128)}, u32[]{:S(2)}) %copy-start.20) | copy-done | bytes 98328
  20.4 0.9 %copy-done.21 = f32[18,8,128]{2,1,0:T(8,128)S(1)} copy-done((f32[18,8,128]{2,1,0:T(8,128)S(1)}, f32[18,8,128]{2,1,0:T(8,128)}, u32[]{:S(2)}) %copy-start.21) | copy-done | bytes 73752
  21.9 50.8 %shard_map.230 = (f32[3,216,128]{2,1,0:T(8,128)S(1)}, f32[216,128]{1,0:T(8,128)S(1)}) custom-call(f32[3,216,128]{2,1,0:T(8,128)S(1)} %copy-done.8, f32[3,216,128]{2,1,0:T(8,128)S(1)} %copy-done.9, f32[216,128]{1,0:T(8,128)S(1)} %copy-done.19, s32[1,128]{1,0:T(1,128)S(1)} %copy-done.22, f32[256,256]{1,0:T(8,128)S(1)} %copy-done.10, ...), custom_call_target="tpu_custom_call" | custom-call | tf_op jit(solution)/shard_map/pallas_call | solution.py:644
  72.7 0.7 copy.27
  (25 shorter events, 1.3 us)
Async XLA Ops:
  0.6 1.0 %copy-start = (bf16[224,768]{1,0:T(8,128)(2,1)S(1)}, bf16[224,768]{1,0:T(8,128)(2,1)}, u32[]{:S(2)}) copy-start(bf16[224,768]{1,0:T(8,128)(2,1)} %constant.43.clone.div_lo) | copy-start | bytes 1032196
  1.6 1.0 %copy-start.1 = (bf16[224,768]{1,0:T(8,128)(2,1)S(1)}, bf16[224,768]{1,0:T(8,128)(2,1)}, u32[]{:S(2)}) copy-start(bf16[224,768]{1,0:T(8,128)(2,1)} %constant.42.clone.div_hi) | copy-start | bytes 1032196
  2.6 1.0 %copy-start.2 = (bf16[224,768]{1,0:T(8,128)(2,1)S(1)}, bf16[224,768]{1,0:T(8,128)(2,1)}, u32[]{:S(2)}) copy-start(bf16[224,768]{1,0:T(8,128)(2,1)} %constant.41.clone.back_lo) | copy-start | bytes 1032196
  3.6 1.0 %copy-start.3 = (bf16[224,768]{1,0:T(8,128)(2,1)S(1)}, bf16[224,768]{1,0:T(8,128)(2,1)}, u32[]{:S(2)}) copy-start(bf16[224,768]{1,0:T(8,128)(2,1)} %constant.40.clone.back_hi) | copy-start | bytes 1032196
  4.5 1.0 %copy-start.4 = (bf16[672,256]{1,0:T(8,128)(2,1)S(1)}, bf16[672,256]{1,0:T(8,128)(2,1)}, u32[]{:S(2)}) copy-start(bf16[672,256]{1,0:T(8,128)(2,1)} %constant.39.clone.cls_lo) | copy-start | bytes 1032196
  5.5 1.0 %copy-start.5 = (bf16[672,256]{1,0:T(8,128)(2,1)S(1)}, bf16[672,256]{1,0:T(8,128)(2,1)}, u32[]{:S(2)}) copy-start(bf16[672,256]{1,0:T(8,128)(2,1)} %constant.38.clone.cls_hi) | copy-start | bytes 1032196
  6.5 1.0 %copy-start.6 = (bf16[672,256]{1,0:T(8,128)(2,1)S(1)}, bf16[672,256]{1,0:T(8,128)(2,1)}, u32[]{:S(2)}) copy-start(bf16[672,256]{1,0:T(8,128)(2,1)} %constant.37.clone.nat_lo) | copy-start | bytes 1032196
  7.5 1.0 %copy-start.7 = (bf16[672,256]{1,0:T(8,128)(2,1)S(1)}, bf16[672,256]{1,0:T(8,128)(2,1)}, u32[]{:S(2)}) copy-start(bf16[672,256]{1,0:T(8,128)(2,1)} %constant.36.clone.nat_hi) | copy-start | bytes 1032196
  8.5 1.0 %copy-start.8 = (f32[3,216,128]{2,1,0:T(8,128)S(1)}, f32[3,216,128]{2,1,0:T(8,128)}, u32[]{:S(2)}) copy-start(f32[3,216,128]{2,1,0:T(8,128)} %vel_ref.1) | copy-start | bytes 995332
  9.4 1.0 %copy-start.9 = (f32[3,216,128]{2,1,0:T(8,128)S(1)}, f32[3,216,128]{2,1,0:T(8,128)}, u32[]{:S(2)}) copy-start(f32[3,216,128]{2,1,0:T(8,128)} %base_ref.1) | copy-start | bytes 995332
  10.4 0.9 %copy-start.10 = (f32[256,256]{1,0:T(8,128)S(1)}, f32[256,256]{1,0:T(8,128)}, u32[]{:S(2)}) copy-start(f32[256,256]{1,0:T(8,128)} %coarse_ref.1) | copy-start | bytes 786436
  11.4 0.9 %copy-start.11 = (bf16[768,128]{1,0:T(8,128)(2,1)S(1)}, bf16[768,128]{1,0:T(8,128)(2,1)}, u32[]{:S(2)}) copy-start(bf16[768,128]{1,0:T(8,128)(2,1)} %constant.53.clone.spread_ref) | copy-start | bytes 589828
  12.3 0.9 %copy-start.12 = (f32[4,7,8,128]{3,2,1,0:T(8,128)S(1)}, f32[4,7,8,128]{3,2,1,0:T(8,128)}, u32[]{:S(2)}) copy-start(f32[4,7,8,128]{3,2,1,0:T(8,128)} %constant.51.clone.side_ref) | copy-start | bytes 344068
  13.2 0.9 %copy-start.13 = (f32[224,128]{1,0:T(8,128)S(1)}, f32[224,128]{1,0:T(8,128)}, u32[]{:S(2)}) copy-start(f32[224,128]{1,0:T(8,128)} %constant.49.clone.pad_ref) | copy-start | bytes 344068
  14.1 0.9 %copy-start.14 = (f32[224,128]{1,0:T(8,128)S(1)}, f32[224,128]{1,0:T(8,128)}, u32[]{:S(2)}) copy-start(f32[224,128]{1,0:T(8,128)} %constant.48.clone.react_ref) | copy-start | bytes 344068
  15.0 0.9 %copy-start.15 = (f32[224,128]{1,0:T(8,128)S(1)}, f32[224,128]{1,0:T(8,128)}, u32[]{:S(2)}) copy-start(f32[224,128]{1,0:T(8,128)} %constant.47.clone.mass_ref) | copy-start | bytes 344068
  15.9 0.9 %copy-start.16 = (bf16[224,256]{1,0:T(8,128)(2,1)S(1)}, bf16[224,256]{1,0:T(8,128)(2,1)}, u32[]{:S(2)}) copy-start(bf16[224,256]{1,0:T(8,128)(2,1)} %constant.46.clone.out_pick) | copy-start | bytes 344068
  16.8 0.9 %copy-start.17 = (bf16[224,256]{1,0:T(8,128)(2,1)S(1)}, bf16[224,256]{1,0:T(8,128)(2,1)}, u32[]{:S(2)}) copy-start(bf16[224,256]{1,0:T(8,128)(2,1)} %constant.45.clone.sq_lo) | copy-start | bytes 344068
  17.7 0.9 %copy-start.18 = (bf16[224,256]{1,0:T(8,128)(2,1)S(1)}, bf16[224,256]{1,0:T(8,128)(2,1)}, u32[]{:S(2)}) copy-start(bf16[224,256]{1,0:T(8,128)(2,1)} %constant.44.clone.sq_hi) | copy-start | bytes 344068
  18.6 0.9 %copy-start.19 = (f32[216,128]{1,0:T(8,128)S(1)}, f32[216,128]{1,0:T(8,128)}, u32[]{:S(2)}) copy-start(f32[216,128]{1,0:T(8,128)} %visc_ref.1) | copy-start | bytes 331780
  19.5 0.9 %copy-start.20 = (f32[3,32,256]{2,1,0:T(8,128)S(1)}, f32[3,32,256]{2,1,0:T(8,128)}, u32[]{:S(2)}) copy-start(f32[3,32,256]{2,1,0:T(8,128)} %constant.52.clone.place_ref) | copy-start | bytes 294916
  20.4 0.9 %copy-start.21 = (f32[18,8,128]{2,1,0:T(8,128)S(1)}, f32[18,8,128]{2,1,0:T(8,128)}, u32[]{:S(2)}) copy-start(f32[18,8,128]{2,1,0:T(8,128)} %constant.50.clone.mask_ref) | copy-start | bytes 221188
  21.3 0.7 copy-start.22

commit v2 on v1

--- a/solution.py
+++ b/solution.py
@@ -330,51 +330,98 @@
     return jnp.sum(jnp.sum(x, axis=0, keepdims=True), axis=2, keepdims=True)
 
 
-def kernel(
-    vel_ref,
-    base_ref,
-    visc_ref,
-    order_ref,
-    coarse_ref,
-    nat_hi,
-    nat_lo,
-    cls_hi,
-    cls_lo,
-    back_hi,
-    back_lo,
-    div_hi,
-    div_lo,
-    sq_hi,
-    sq_lo,
-    out_pick,
-    mass_ref,
-    react_ref,
-    pad_ref,
-    mask_ref,
-    side_ref,
-    place_ref,
-    spread_ref,
-    lin_ref,
-    press_ref,
-    field,
-    y_up,
-    y_down,
-    got_x,
-    got_y,
-    got_c,
-    row_a,
-    row_b,
-    all_a,
-    all_b,
-    weight_ref,
-    solve_ref,
-    send_h,
-    recv_h,
-    send_a,
-    recv_a,
-    send_b,
-    recv_b,
-):
+NAMES = (
+    "vel",
+    "base",
+    "visc",
+    "order",
+    "coarse",
+    "nat_hi",
+    "nat_lo",
+    "cls_hi",
+    "cls_lo",
+    "back_hi",
+    "back_lo",
+    "div_hi",
+    "div_lo",
+    "sq_hi",
+    "sq_lo",
+    "out_pick",
+    "mass",
+    "react",
+    "pad",
+    "mask",
+    "side",
+    "place",
+    "spread",
+)
+ORDER = (
+    "nat_hi",
+    "vel",
+    "base",
+    "nat_lo",
+    "div_hi",
+    "div_lo",
+    "order",
+    "visc",
+    "mask",
+    "side",
+    "mass",
+    "sq_hi",
+    "sq_lo",
+    "react",
+    "coarse",
+    "place",
+    "spread",
+    "pad",
+    "cls_hi",
+    "cls_lo",
+    "back_hi",
+    "back_lo",
+    "out_pick",
+)
+
+
+def kernel(*refs):
+    count = len(NAMES)
+    sources = dict(zip(NAMES, refs[:count]))
+    lin_ref, press_ref = refs[count : count + 2]
+    held = dict(zip(NAMES, refs[count + 2 : 2 * count + 2]))
+    (
+        load_sem,
+        field,
+        y_up,
+        y_down,
+        got_x,
+        got_y,
+        got_c,
+        row_a,
+        row_b,
+        all_a,
+        all_b,
+        weight_ref,
+        solve_ref,
+        send_h,
+        recv_h,
+        send_a,
+        recv_a,
+        send_b,
+        recv_b,
+    ) = refs[2 * count + 2 :]
+    loads = {
+        name: pltpu.make_async_copy(sources[name], held[name], load_sem.at[at])
+        for at, name in enumerate(NAMES)
+    }
+    for name in ORDER:
+        loads[name].start()
+    ready = set()
+
+    def need(name):
+        if name not in ready:
+            loads[name].wait()
+            ready.add(name)
+        return held[name]
+
     dom = lax.axis_index("dom")
     sub = lax.axis_index("sub")
     dom_next, dom_prev = lax.rem(dom + 1, DOM), lax.rem(dom + DOM - 1, DOM)
@@ -397,18 +444,18 @@
     for where in diagonals:
         greet(where)
 
-    mask = lambda at: mask_ref[at]
+    mask = lambda at: need("mask")[at]
 
     def flag(condition):
         return jnp.where(condition, 1.0, 0.0).astype(F32)
 
     has = (flag(dom > 0), flag(dom < DOM - 1), flag(sub > 0), flag(sub < SUB - 1))
 
-    vel = [pad_rows(vel_ref[c], ROWS) for c in range(3)]
-    base = [pad_rows(base_ref[c], ROWS) for c in range(3)]
+    vel = [pad_rows(need("vel")[c], ROWS) for c in range(3)]
+    base = [pad_rows(need("base")[c], ROWS) for c in range(3)]
     advect = []
     for c in range(3):
-        grads = product(nat_hi, nat_lo, jnp.concatenate([vel[c], base[c]], axis=1))
+        grads = product(need("nat_hi"), need("nat_lo"), jnp.concatenate([vel[c], base[c]], axis=1))
         acc = jnp.zeros((ROWS, 128), F32)
         for m in range(3):
             part = grads[ROWS * m : ROWS * (m + 1)]
@@ -416,13 +463,13 @@
         advect.append(acc)
         lin_ref[c] = acc[:NAT]
     select = jnp.where(
-        lax.broadcasted_iota(jnp.int32, (128, 128), 0) == order_ref[...], 1.0, 0.0
+        lax.broadcasted_iota(jnp.int32, (128, 128), 0) == need("order")[...], 1.0, 0.0
     ).astype(BF16)
     moved = move_lanes(
         jnp.concatenate(
             [
-                product(div_hi, div_lo, jnp.concatenate(advect, axis=0)),
-                pad_rows(visc_ref[...], ROWS),
+                product(need("div_hi"), need("div_lo"), jnp.concatenate(advect, axis=0)),
+                pad_rows(need("visc")[...], ROWS),
             ],
             axis=0,
         ),
@@ -430,13 +477,13 @@
         True,
     )
     rhs_own = cube(moved[:ROWS])
-    weighted = mass_ref[...] * moved[ROWS:]
+    weighted = need("mass")[...] * moved[ROWS:]
     weight_ref[...] = jnp.concatenate([weighted, weighted, weighted], axis=0)
-    diag_own = cube(react_ref[...] + product(sq_hi, sq_lo, weighted))
+    diag_own = cube(need("react")[...] + product(need("sq_hi"), need("sq_lo"), weighted))
 
     left, right, down, up = has
-    side_l, side_r = (0.5 * left) * side_ref[0], (0.5 * right) * side_ref[1]
-    side_d, side_u = (0.5 * down) * side_ref[2], (0.5 * up) * side_ref[3]
+    side_l, side_r = (0.5 * left) * need("side")[0], (0.5 * right) * need("side")[1]
+    side_d, side_u = (0.5 * down) * need("side")[2], (0.5 * up) * need("side")[3]
     along_x = (side_l, 1.0 - side_l - side_r, side_r)
     along_y = (side_d, 1.0 - side_d - side_u, side_u)
 
@@ -542,9 +589,9 @@
 
     def apply(u):
         v = flat(u)
-        g = product(cls_hi, cls_lo, v)
+        g = product(need("cls_hi"), need("cls_lo"), v)
         h = pad_rows(g * weight_ref[...], 768)
-        return cube(product(back_hi, back_lo, h) + react_ref[...] * v)
+        return cube(product(need("back_hi"), need("back_lo"), h) + need("react")[...] * v)
 
     def inner(a, b):
         return jnp.sum(a * b, axis=0, keepdims=True)
@@ -571,16 +618,16 @@
     for ax in (-1, 0, 1):
         for ay in (-1, 0, 1):
             at = jnp.clip((dom + ax) * SUB + sub + ay, 0, DOM * SUB - 1)
-            chosen.append(coarse_ref[pl.ds(at, 1), :])
+            chosen.append(need("coarse")[pl.ds(at, 1), :])
     for a in range(NFACE):
-        wide = jnp.concatenate([place_ref[fx] * chosen[a] for fx in range(3)], axis=1)
+        wide = jnp.concatenate([need("place")[fx] * chosen[a] for fx in range(3)], axis=1)
         pieces = thirds(wide)
-        solve_ref[a] = sum(dot(piece, spread_ref[...]) for piece in pieces)
+        solve_ref[a] = sum(dot(piece, need("spread")[...]) for piece in pieces)
 
     forward_gather(0, row)
     r_all = finish_halo(0, 0, rhs_block)
     d_all = finish_halo(1, 1, diag_block)
-    inverse = 1.0 / (d_all + cube(pad_ref[...]))
+    inverse = 1.0 / (d_all + cube(need("pad")[...]))
     solved = results(finish_gather(0), 0)
     r_own = rhs_own
     z = inverse * r_all + spread_coarse(solved)
@@ -623,8 +670,8 @@
             z = inverse * r_all + spread_coarse(solved)
 
     slots = pad_rows(move_lanes(flat(q), select, False), 256)
-    press_ref[...] = sum(dot(out_pick[...], piece) for piece in thirds(slots))[:NAT]
-    grads = product(cls_hi, cls_lo, slots)
+    press_ref[...] = sum(dot(need("out_pick")[...], piece) for piece in thirds(slots))[:NAT]
+    grads = product(need("cls_hi"), need("cls_lo"), slots)
     for c in range(3):
         lin_ref[c] = lin_ref[c] - grads[ROWS * c : ROWS * c + NAT]
 
@@ -640,6 +687,7 @@
     args = [velocity, base_flow, viscosity, cell_order, coarse_inv]
     args += [jnp.asarray(t) for t in tables()]
     vmem = pl.BlockSpec(memory_space=pltpu.VMEM)
+    hbm = pl.BlockSpec(memory_space=pltpu.HBM)
     dma = pltpu.SemaphoreType.DMA
     return pl.pallas_call(
         kernel,
@@ -647,9 +695,11 @@
             jax.ShapeDtypeStruct((3, NAT, 128), F32),
             jax.ShapeDtypeStruct((NAT, 128), F32),
         ),
-        in_specs=[vmem] * len(args),
+        in_specs=[hbm] * len(args),
         out_specs=(vmem, vmem),
-        scratch_shapes=[
+        scratch_shapes=[pltpu.VMEM(arg.shape, arg.dtype) for arg in args]
+        + [
+            dma((len(args),)),
             pltpu.VMEM((4, 28, 8, 128), F32),
             pltpu.VMEM((4, 7, 8, 128), F32),
             pltpu.VMEM((4, 7, 8, 128), F32),
@@ -670,7 +720,7 @@
             dma((4,)),
         ],
         compiler_params=pltpu.CompilerParams(
-            collective_id=0, has_side_effects=True, vmem_limit_bytes=48 << 20
+            collective_id=0, has_side_effects=True, vmem_limit_bytes=62 << 20
         ),
     )(*args)
 

time: 74.9 us -> 55.4 us (0.74)
  local copies, waits for them, and re-layouts: 22.6 us -> 2.4 us
  Pallas kernels: 50.8 us -> 52.2 us
    unnamed x48 -> x4, local copies, waits for them, and re-layouts: 22.6 us -> 2.4 us
    pallas_call x1, Pallas kernels: 50.8 us -> 52.2 us  [shards(): pl.pallas_call(kernel, out_shape=(jax.ShapeDtypeStruct((3, NAT, 128), F32...]
where the time goes in v2:
time: 55.4 us; the launch traced here: 55.3 us
  Pallas kernels  52.2 us (94%)
  local copies, waits for them, and re-layouts  2.4 us (4%)
  between operations  0.65 us (1%)
    pallas_call x1, Pallas kernels, shards(): pl.pallas_call(kernel, out_shape=(jax.ShapeDtypeStruct((3, NAT, 128), F32...  52.2 us
    unnamed x4, local copies, waits for them, and re-layouts  2.4 us

profile of v2, /device:TPU:1, one launch (start us, length us, event | category | flops | bytes accessed | tf_op | source)
XLA Modules:
  0.0 55.3 jit_solution(15975069788916142683)
XLA Ops:
  0.6 52.2 %shard_map.230 = (f32[3,216,128]{2,1,0:T(8,128)}, f32[216,128]{1,0:T(8,128)}) custom-call(f32[3,216,128]{2,1,0:T(8,128)} %refs_0_.1, f32[3,216,128]{2,1,0:T(8,128)} %refs_1_.1, f32[216,128]{1,0:T(8,128)} %refs_2_.1, s32[1,128]{1,0:T(1,128)} %refs_3_.1, f32[256,256]{1,0:T(8,128)} %refs_4_.1, bf16[672,256]{1,0:T(8,128)(2,1)} %constant.36.clone.refs_5_, ...), custom_call_target="tpu_custom_call" | custom-call | tf_op jit(solution)/shard_map/pallas_call | solution.py:692
  52.9 0.0 copy-start
  52.9 1.8 %copy.27 = f32[3,216,128]{2,1,0:T(8,128)} copy(f32[3,216,128]{2,1,0:T(8,128)} %get-tuple-element.4) | data formatting | bytes 663552
  54.6 0.0 copy-done
  54.6 0.6 %copy.28 = f32[216,128]{1,0:T(8,128)} copy(f32[216,128]{1,0:T(8,128)S(1)} %copy-done) | data formatting | bytes 221184
Async XLA Ops:
  52.9 1.8 %copy-start = (f32[216,128]{1,0:T(8,128)S(1)}, f32[216,128]{1,0:T(8,128)}, u32[]{:S(2)}) copy-start(f32[216,128]{1,0:T(8,128)} %get-tuple-element.5) | copy-start | bytes 331780

commit v3 on v2

--- a/solution.py
+++ b/solution.py
@@ -15,6 +15,7 @@
 REACTION = 0.001
 DOM = 32
 SUB = 8
+CHIPS = 128
 ROWS = 224
 NAT = 216
 NFACE = 9
@@ -431,10 +432,32 @@
     def greet(where):
         pl.semaphore_signal(barrier, inc=1, device_id=where, device_id_type=MESH)
 
-    for step in range(1, SUB):
-        greet((dom, lax.rem(sub + step, SUB)))
-    for step in range(1, DOM):
-        greet((lax.rem(dom + step, DOM), sub))
+    core = lax.rem(sub, 2)
+    chip_x = lax.div(sub, 2)
+    chip_y = lax.div(dom, 8)
+    chip_z = lax.rem(dom, 8)
+    row_starts = [8 * lax.rem(chip_y + step, 4) for step in (2, 1, 3, 0)]
+    columns = [lax.rem(sub + 2 * step, SUB) for step in (2, 1, 3, 0)]
+
+    def each_chip(visit):
+        @pl.loop(0, 7)
+        def _(n):
+            step = 4 + (1 - 2 * lax.rem(n, 2)) * lax.div(n + 1, 2)
+            z = lax.rem(chip_z + step, 8)
+            for start in row_starts:
+                for column in columns:
+                    visit((start + z, column))
+
+        for start in row_starts:
+            for column in columns:
+                if start is not row_starts[3] or column is not columns[3]:
+                    visit((start + chip_z, column))
+
+    partner = (dom, sub + 1 - 2 * core)
+
+    each_chip(greet)
+    greet(partner)
+    greet((dom, jnp.where(core == 0, sub_prev, sub_next)))
     diagonals = (
         (dom_prev, sub_prev),
         (dom_prev, sub_next),
@@ -526,33 +549,25 @@
             sums = jnp.concatenate([sums, jnp.zeros((16 - count, 1), F32)], axis=0)
         row = jnp.sum(jnp.where(home, sums, 0.0), axis=0, keepdims=True)
         row_a[at] = row
-        for step in range(1, SUB):
-            send(
-                row_a.at[at],
-                all_a.at[at, step - 1],
-                send_a.at[at],
-                recv_a.at[at],
-                (dom, lax.rem(sub + step, SUB)),
-            )
+        send(row_a.at[at], all_a.at[at], send_a.at[at], recv_a.at[at], partner)
         return row
 
     def forward_gather(at, row):
         wait_for(all_a.at[at], recv_a.at[at])
-        row = row + jnp.sum(all_a[at], axis=0)
+        row = row + all_a[at]
         row_b[at] = row
-        for step in range(1, DOM):
-            send(
-                row_b.at[at],
-                all_b.at[at, dom],
-                send_b.at[at],
-                recv_b.at[at],
-                (lax.rem(dom + step, DOM), sub),
+        here = DOM * chip_x + dom
+
+        each_chip(
+            functools.partial(
+                send, row_b.at[at], all_b.at[at, here], send_b.at[at], recv_b.at[at]
             )
-        all_b[at, dom] = row
+        )
+        all_b[at, here] = row
 
     def finish_gather(at):
-        wait_for(all_b.at[at, 0 : DOM - 1], recv_b.at[at])
-        return all_b[at].reshape(DOM, 128)
+        wait_for(all_b.at[at, 0 : CHIPS - 1], recv_b.at[at])
+        return jnp.sum(all_b[at].reshape(4, DOM, 128), axis=0)
 
     def start_halo(at, which, own):
         t = block_sum(own, mask)
@@ -609,7 +624,7 @@
         )
         return [sums[n] for n in range(NFACE + dots)]
 
-    pl.semaphore_wait(barrier, SUB - 1 + DOM - 1 + 4)
+    pl.semaphore_wait(barrier, CHIPS - 1 + 2 + 4)
     row = start_gather(0, coarse_parts(by_kind(rhs_own)))
     rhs_block = start_halo(0, 0, rhs_own)
     diag_block = start_halo(1, 1, diag_own)
@@ -677,7 +692,7 @@
 
     for at in range(4):
         wait_for(all_a.at[at], send_a.at[at])
-        wait_for(all_b.at[at, 0 : DOM - 1], send_b.at[at])
+        wait_for(all_b.at[at, 0 : CHIPS - 1], send_b.at[at])
         wait_for(got_x.at[at], send_h.at[at, 0])
         wait_for(got_y.at[at], send_h.at[at, 1])
         wait_for(got_c.at[at], send_h.at[at, 2])
@@ -692,8 +707,8 @@
     return pl.pallas_call(
         kernel,
         out_shape=(
-            jax.ShapeDtypeStruct((3, NAT, 128), F32),
-            jax.ShapeDtypeStruct((NAT, 128), F32),
+            pltpu.VMEM((3, NAT, 128), F32),
+            pltpu.VMEM((NAT, 128), F32),
         ),
         in_specs=[hbm] * len(args),
         out_specs=(vmem, vmem),
@@ -708,8 +723,8 @@
             pltpu.VMEM((4, 4, 2, 8, 128), F32),
             pltpu.VMEM((4, 1, 128), F32),
             pltpu.VMEM((4, 1, 128), F32),
-            pltpu.VMEM((4, SUB - 1, 1, 128), F32),
-            pltpu.VMEM((4, DOM, 1, 128), F32),
+            pltpu.VMEM((4, 1, 128), F32),
+            pltpu.VMEM((4, CHIPS, 1, 128), F32),
             pltpu.VMEM((3 * ROWS, 128), F32),
             pltpu.VMEM((NFACE, DOM, 128), F32),
             dma((4, 3)),
@@ -720,9 +735,9 @@
             dma((4,)),
         ],
         compiler_params=pltpu.CompilerParams(
-            collective_id=0, has_side_effects=True, vmem_limit_bytes=62 << 20
+            collective_id=0, has_side_effects=True, vmem_limit_bytes=40 << 20
         ),
-    )(*args)
+    )(*[pltpu.with_memory_space_constraint(arg, pltpu.HBM) for arg in args])
 
 
 def solution(mesh):

time: 55.4 us -> 51 us (0.921)
  Pallas kernels: 52.2 us -> 48.9 us
  local copies, waits for them, and re-layouts: 2.4 us -> 1.37 us
    pallas_call x1, Pallas kernels: 52.2 us -> 48.9 us  [shards(): pl.pallas_call(kernel, out_shape=(pltpu.VMEM((3, NAT, 128), F32), pltpu.V...]
    unnamed x4 -> x2, local copies, waits for them, and re-layouts: 2.4 us -> 1.37 us
where the time goes in v3:
time: 51 us; the launch traced here: 50.9 us
  Pallas kernels  48.9 us (96%)
  local copies, waits for them, and re-layouts  1.37 us (3%)
  between operations  0.64 us (1%)
    pallas_call x1, Pallas kernels, shards(): pl.pallas_call(kernel, out_shape=(pltpu.VMEM((3, NAT, 128), F32), pltpu.V...  48.9 us
    unnamed x2, local copies, waits for them, and re-layouts  1.37 us

profile of v3, /device:TPU:1, one launch (start us, length us, event | category | flops | bytes accessed | tf_op | source)
XLA Modules:
  0.0 50.9 jit_solution(10986579711502663014)
XLA Ops:
  0.6 48.9 %shard_map.230 = (f32[3,216,128]{2,1,0:T(8,128)S(1)}, f32[216,128]{1,0:T(8,128)S(1)}) custom-call(f32[3,216,128]{2,1,0:T(8,128)} %refs_0_.1, f32[3,216,128]{2,1,0:T(8,128)} %refs_1_.1, f32[216,128]{1,0:T(8,128)} %refs_2_.1, s32[1,128]{1,0:T(1,128)} %refs_3_.1, f32[256,256]{1,0:T(8,128)} %refs_4_.1, bf16[672,256]{1,0:T(8,128)(2,1)} %constant.36.clone.refs_5_, ...), custom_call_target="tpu_custom_call" | custom-call | tf_op jit(solution)/shard_map/pallas_call | solution.py:707
  49.6 0.7 %copy.27 = f32[3,216,128]{2,1,0:T(8,128)} copy(f32[3,216,128]{2,1,0:T(8,128)S(1)} %get-tuple-element.2) | data formatting | bytes 663552
  50.3 0.6 %copy.28 = f32[216,128]{1,0:T(8,128)} copy(f32[216,128]{1,0:T(8,128)S(1)} %get-tuple-element.3) | data formatting | bytes 221184

commit v4 on v3

--- a/solution.py
+++ b/solution.py
@@ -19,6 +19,7 @@
 ROWS = 224
 NAT = 216
 NFACE = 9
+MESSAGE_ROWS = (1, 1, 2, 2)
 
 
 def gll_tables():
@@ -175,8 +176,31 @@
             & ((column % 8)[:, None] == (lanes // 16 + f % 3 - 1)[None, :])
         )
     out.append(place.astype(np.float32))
+    pairs = coarse_pairs()
+    firsts = np.zeros((3, 256, 256))
+    seconds = np.zeros((3, 256, 256))
+    slots = np.full((2, 88, 128), -1000, np.int32)
+    for at, (f, g) in enumerate(pairs):
+        group, inside = at // 16, at % 16
+        slots[group, 9 * f + g] = inside
+        for sub in range(SUB):
+            column_at = 128 * group + 16 * sub + inside
+            firsts[f // 3, :, column_at] = ((column % 8) == sub + f % 3 - 1) * (1 + (f != g))
+            seconds[g // 3, :, column_at] = (column % 8) == sub + g % 3 - 1
+    unfold = np.concatenate([spread, firsts, seconds], axis=2)
     out.append(spread.reshape(768, 128).astype(ml_dtypes.bfloat16))
+    out.append(unfold.reshape(768, 640).astype(ml_dtypes.bfloat16))
+    out.append(slots)
     return out
+
+
+def coarse_pairs():
+    return [
+        (f, g)
+        for f in range(NFACE)
+        for g in range(f, NFACE)
+        if abs(f // 3 - g // 3) < 2 and abs(f % 3 - g % 3) < 2
+    ]
 
 
 def dot(a, b):
@@ -355,6 +379,8 @@
     "side",
     "place",
     "spread",
+    "unfold",
+    "slots",
 )
 ORDER = (
     "nat_hi",
@@ -379,6 +405,8 @@
     "cls_lo",
     "back_hi",
     "back_lo",
+    "unfold",
+    "slots",
     "out_pick",
 )
 
@@ -396,12 +424,28 @@
         got_x,
         got_y,
         got_c,
-        row_a,
-        row_b,
-        all_a,
-        all_b,
+        row_a0,
+        row_a1,
+        row_a2,
+        row_a3,
+        row_b0,
+        row_b1,
+        row_b2,
+        row_b3,
+        all_a0,
+        all_a1,
+        all_a2,
+        all_a3,
+        all_b0,
+        all_b1,
+        all_b2,
+        all_b3,
         weight_ref,
         solve_ref,
+        phi_ref,
+        entry_ref,
+        coarse_hi,
+        coarse_lo,
         send_h,
         recv_h,
         send_a,
@@ -409,11 +453,15 @@
         send_b,
         recv_b,
     ) = refs[2 * count + 2 :]
+    row_a = (row_a0, row_a1, row_a2, row_a3)
+    row_b = (row_b0, row_b1, row_b2, row_b3)
+    all_a = (all_a0, all_a1, all_a2, all_a3)
+    all_b = (all_b0, all_b1, all_b2, all_b3)
     loads = {
         name: pltpu.make_async_copy(sources[name], held[name], load_sem.at[at])
         for at, name in enumerate(NAMES)
     }
-    for name in ORDER:
+    for name in ORDER[:4]:
         loads[name].start()
     ready = set()
 
@@ -466,6 +514,8 @@
     )
     for where in diagonals:
         greet(where)
+    for name in ORDER[4:]:
+        loads[name].start()
 
     mask = lambda at: need("mask")[at]
 
@@ -488,21 +538,11 @@
     select = jnp.where(
         lax.broadcasted_iota(jnp.int32, (128, 128), 0) == need("order")[...], 1.0, 0.0
     ).astype(BF16)
-    moved = move_lanes(
-        jnp.concatenate(
-            [
-                product(need("div_hi"), need("div_lo"), jnp.concatenate(advect, axis=0)),
-                pad_rows(need("visc")[...], ROWS),
-            ],
-            axis=0,
-        ),
-        select,
-        True,
-    )
-    rhs_own = cube(moved[:ROWS])
-    weighted = need("mass")[...] * moved[ROWS:]
-    weight_ref[...] = jnp.concatenate([weighted, weighted, weighted], axis=0)
-    diag_own = cube(need("react")[...] + product(need("sq_hi"), need("sq_lo"), weighted))
+    rhs_own = cube(
+        move_lanes(
+            product(need("div_hi"), need("div_lo"), jnp.concatenate(advect, axis=0)), select, True
+        )
+    )
 
     left, right, down, up = has
     side_l, side_r = (0.5 * left) * need("side")[0], (0.5 * right) * need("side")[1]
@@ -541,33 +581,39 @@
     def wait_for(ref, sem):
         pltpu.make_async_copy(ref, ref, sem).wait()
 
-    def start_gather(at, partials):
+    def packed(partials):
         count = len(partials)
         stack = jnp.concatenate(partials, axis=0)
         sums = jnp.sum(jnp.sum(stack, axis=1), axis=1, keepdims=True)
         if count < 16:
             sums = jnp.concatenate([sums, jnp.zeros((16 - count, 1), F32)], axis=0)
-        row = jnp.sum(jnp.where(home, sums, 0.0), axis=0, keepdims=True)
-        row_a[at] = row
-        send(row_a.at[at], all_a.at[at], send_a.at[at], recv_a.at[at], partner)
-        return row
-
-    def forward_gather(at, row):
-        wait_for(all_a.at[at], recv_a.at[at])
-        row = row + all_a[at]
-        row_b[at] = row
+        return jnp.sum(jnp.where(home, sums, 0.0), axis=0, keepdims=True)
+
+    def start_gather(at, rows):
+        for n, row in enumerate(rows):
+            row_a[at][n] = row
+        send(row_a[at], all_a[at], send_a.at[at], recv_a.at[at], partner)
+
+    def forward_gather(at, rows):
+        wait_for(all_a[at], recv_a.at[at])
         here = DOM * chip_x + dom
-
+        rows = [row + all_a[at][n] for n, row in enumerate(rows)]
+        for n, row in enumerate(rows):
+            row_b[at][n] = row
         each_chip(
             functools.partial(
-                send, row_b.at[at], all_b.at[at, here], send_b.at[at], recv_b.at[at]
+                send, row_b[at], all_b[at].at[here], send_b.at[at], recv_b.at[at]
             )
         )
-        all_b[at, here] = row
+        for n, row in enumerate(rows):
+            all_b[at][here, n] = row
 
     def finish_gather(at):
-        wait_for(all_b.at[at, 0 : CHIPS - 1], recv_b.at[at])
-        return jnp.sum(all_b[at].reshape(4, DOM, 128), axis=0)
+        wait_for(all_b[at].at[0 : CHIPS - 1], recv_b.at[at])
+        return [
+            jnp.sum(all_b[at][:, n].reshape(4, DOM, 128), axis=0)
+            for n in range(all_b[at].shape[1])
+        ]
 
     def start_halo(at, which, own):
         t = block_sum(own, mask)
@@ -625,7 +671,12 @@
         return [sums[n] for n in range(NFACE + dots)]
 
     pl.semaphore_wait(barrier, CHIPS - 1 + 2 + 4)
-    row = start_gather(0, coarse_parts(by_kind(rhs_own)))
+    rows = [packed(coarse_parts(by_kind(rhs_own)))]
+    start_gather(0, rows)
+    weighted = need("mass")[...] * move_lanes(pad_rows(need("visc")[...], ROWS), select, True)
+    weight_ref[...] = jnp.concatenate([weighted, weighted, weighted], axis=0)
+    diag_own = cube(need("react")[...] + product(need("sq_hi"), need("sq_lo"), weighted))
+    forward_gather(0, rows)
     rhs_block = start_halo(0, 0, rhs_own)
     diag_block = start_halo(1, 1, diag_own)
 
@@ -636,53 +687,124 @@
             chosen.append(need("coarse")[pl.ds(at, 1), :])
     for a in range(NFACE):
         wide = jnp.concatenate([need("place")[fx] * chosen[a] for fx in range(3)], axis=1)
-        pieces = thirds(wide)
-        solve_ref[a] = sum(dot(piece, need("spread")[...]) for piece in pieces)
-
-    forward_gather(0, row)
+        solve_ref[a] = sum(dot(piece, need("spread")[...]) for piece in thirds(wide))
+    coarse_hi[...], coarse_lo[...] = halves(need("coarse")[...])
+
+    for fx in range(3):
+        for fy in range(3):
+            phi_ref[3 * fx + fy] = from_kinds(along_x[fx] * along_y[fy])
+    need("cls_hi"), need("cls_lo"), need("back_hi"), need("back_lo")
+
+    def coarse_entries(first, last):
+        @pl.loop(first, last)
+        def _(f):
+            entry_ref[f] = jnp.concatenate(coarse_parts(by_kind(apply(phi_ref[f]))), axis=0)
+
+    coarse_entries(0, 5)
     r_all = finish_halo(0, 0, rhs_block)
     d_all = finish_halo(1, 1, diag_block)
     inverse = 1.0 / (d_all + cube(need("pad")[...]))
-    solved = results(finish_gather(0), 0)
-    r_own = rhs_own
-    z = inverse * r_all + spread_coarse(solved)
-
-    direction = None
-    for it in range(3):
-        w_own = apply(z)
-        dots = [inner(z, r_own), inner(z, w_own)]
-        last = it == 2
-        parts = coarse_parts(by_kind(w_own)) if not last else [jnp.zeros((1, 8, 128), F32)] * 9
-        row = start_gather(it + 1, parts + dots)
-        if not last:
-            w_block = start_halo(it + 2, it + 2, w_own)
-        forward_gather(it + 1, row)
-        if not last:
-            w_all = finish_halo(it + 2, it + 2, w_block)
-        got = results(finish_gather(it + 1), 2)
-        gamma, curve = got[NFACE], got[NFACE + 1]
-        solved_w = got[:NFACE]
-        if it == 0:
-            alpha = gamma / curve
-            direction = z
-            q = alpha * direction
-            if not last:
-                along_own, along_all, along_solved = w_own, w_all, solved_w
-        else:
-            beta = gamma / gamma_before
-            alpha = gamma / (curve - beta * gamma / alpha)
-            direction = z + beta * direction
-            q = q + alpha * direction
-            if not last:
-                along_own = w_own + beta * along_own
-                along_all = w_all + beta * along_all
-                along_solved = [a + beta * b for a, b in zip(solved_w, along_solved)]
-        gamma_before = gamma
-        if not last:
-            r_own = r_own - alpha * along_own
-            r_all = r_all - alpha * along_all
-            solved = [a - alpha * b for a, b in zip(solved, along_solved)]
-            z = inverse * r_all + spread_coarse(solved)
+    solved = results(finish_gather(0)[0], 0)
+    z0 = inverse * r_all + spread_coarse(solved)
+
+    w0 = apply(z0)
+    rows = [
+        packed(coarse_parts(by_kind(w0)) + [inner(z0, rhs_own), inner(z0, w0)])
+    ]
+    start_gather(1, rows)
+    w_block = start_halo(2, 2, w0)
+    forward_gather(1, rows)
+    coarse_entries(5, NFACE)
+    sums = jnp.sum(jnp.sum(entry_ref[...].reshape(81, 8, 128), axis=1), axis=1, keepdims=True)
+    sums = jnp.concatenate([sums, jnp.zeros((7, 1), F32)], axis=0)
+    lanes = lax.broadcasted_iota(jnp.int32, (88, 128), 1)
+    rows = [
+        jnp.sum(
+            jnp.where(lanes == 16 * sub + need("slots")[n], sums, 0.0), axis=0, keepdims=True
+        )
+        for n in range(2)
+    ]
+    start_gather(2, rows)
+    forward_gather(2, rows)
+    w0_all = finish_halo(2, 2, w_block)
+    got = results(finish_gather(1)[0], 2)
+    gamma0 = got[NFACE]
+    alpha0 = gamma0 / got[NFACE + 1]
+    m0 = inverse * w0_all + spread_coarse(got[:NFACE])
+    z1 = z0 - alpha0 * m0
+    r1 = rhs_own - alpha0 * w0
+
+    w1 = apply(z1)
+    w_block = start_halo(3, 3, w1)
+    parts = coarse_parts(by_kind(w1)) + [
+        inner(z1, r1),
+        inner(z1, w1),
+        inner(z1, w0),
+        inner(m0, w1),
+        inner(m0, w0),
+    ]
+    y = inverse * finish_halo(3, 3, w_block)
+    t = apply(y)
+    rows = [
+        packed(parts + [inner(y, w1), inner(y, t)]),
+        packed(coarse_parts(by_kind(t))),
+    ]
+    start_gather(3, rows)
+    forward_gather(3, rows)
+    entries = finish_gather(2)
+    place = jnp.concatenate([need("place")[fx] for fx in range(3)], axis=1)
+    every_w, every_t = finish_gather(3)
+    got = results(every_w, 7)
+    gamma1, z1w1, z1w0, m0w1, m0w0, yw1, yt = got[NFACE:]
+
+    folded = lax.dot_general(
+        jnp.concatenate(thirds(every_w), axis=0),
+        need("spread")[...],
+        (((1,), (1,)), ((), ())),
+        preferred_element_type=F32,
+    )
+    folded = folded[:DOM] + folded[DOM : 2 * DOM] + folded[2 * DOM :]
+    folded = jnp.sum(folded * place, axis=0, keepdims=True)
+    folded = folded[:, :256] + folded[:, 256:512] + folded[:, 512:]
+    high, low = halves(jnp.concatenate([folded, jnp.zeros((15, 256), F32)], axis=0))
+    second = (
+        dot(high, coarse_hi[...]) + dot(high, coarse_lo[...]) + dot(low, coarse_hi[...])
+    )[0:1]
+    wide = place * jnp.concatenate([second, second, second], axis=1)
+    unfolded = dot(jnp.concatenate(thirds(wide), axis=0), need("unfold")[...])
+    unfolded = unfolded[:DOM] + unfolded[DOM : 2 * DOM] + unfolded[2 * DOM :]
+    chat = unfolded[:, :128]
+    quad = sum(
+        unfolded[:, 128 * (1 + n) : 128 * (2 + n)]
+        * unfolded[:, 128 * (3 + n) : 128 * (4 + n)]
+        * entries[n]
+        for n in range(2)
+    )
+
+    def total(x):
+        return jnp.sum(jnp.sum(x, axis=0, keepdims=True), axis=1, keepdims=True)
+
+    m1w1 = yw1 + total(chat * every_w)
+    m1am1 = yt + total(2.0 * (chat * every_t) + quad)
+    beta0 = gamma1 / gamma0
+    alpha1 = gamma1 / (z1w1 - beta0 * gamma1 / alpha0)
+    gamma2 = (
+        gamma1
+        - 2.0 * alpha1 * (z1w1 + beta0 * z1w0)
+        + alpha1 * alpha1 * (m1w1 + beta0 * (2.0 * m0w1 + beta0 * m0w0))
+    )
+    curve2 = (
+        z1w1
+        - 2.0 * alpha1 * (m1w1 + beta0 * m0w1)
+        + alpha1
+        * alpha1
+        * (m1am1 + beta0 / alpha0 * (2.0 * (m0w1 - m1w1) + beta0 * (m0w0 - m0w1)))
+    )
+    beta1 = gamma2 / gamma1
+    alpha2 = gamma2 / (curve2 - beta1 * gamma2 / alpha1)
+    z2 = z1 - alpha1 * (y + spread_coarse(got[:NFACE]) + beta0 * m0)
+    p1 = z1 + beta0 * z0
+    q = alpha0 * z0 + alpha1 * p1 + alpha2 * (z2 + beta1 * p1)
 
     slots = pad_rows(move_lanes(flat(q), select, False), 256)
     press_ref[...] = sum(dot(need("out_pick")[...], piece) for piece in thirds(slots))[:NAT]
@@ -691,8 +813,8 @@
         lin_ref[c] = lin_ref[c] - grads[ROWS * c : ROWS * c + NAT]
 
     for at in range(4):
-        wait_for(all_a.at[at], send_a.at[at])
-        wait_for(all_b.at[at, 0 : CHIPS - 1], send_b.at[at])
+        wait_for(all_a[at], send_a.at[at])
+        wait_for(all_b[at].at[0 : CHIPS - 1], send_b.at[at])
         wait_for(got_x.at[at], send_h.at[at, 0])
         wait_for(got_y.at[at], send_h.at[at, 1])
         wait_for(got_c.at[at], send_h.at[at, 2])
@@ -721,12 +843,16 @@
             pltpu.VMEM((4, 2, 5, 8, 128), F32),
             pltpu.VMEM((4, 2, 7, 8, 128), F32),
             pltpu.VMEM((4, 4, 2, 8, 128), F32),
-            pltpu.VMEM((4, 1, 128), F32),
-            pltpu.VMEM((4, 1, 128), F32),
-            pltpu.VMEM((4, 1, 128), F32),
-            pltpu.VMEM((4, CHIPS, 1, 128), F32),
+        ]
+        + 3 * [pltpu.VMEM((n, 1, 128), F32) for n in MESSAGE_ROWS]
+        + [pltpu.VMEM((CHIPS, n, 1, 128), F32) for n in MESSAGE_ROWS]
+        + [
             pltpu.VMEM((3 * ROWS, 128), F32),
             pltpu.VMEM((NFACE, DOM, 128), F32),
+            pltpu.VMEM((NFACE, 28, 8, 128), F32),
+            pltpu.VMEM((NFACE, NFACE, 8, 128), F32),
+            pltpu.VMEM((256, 256), BF16),
+            pltpu.VMEM((256, 256), BF16),
             dma((4, 3)),
             dma((4, 3)),
             dma((4,)),

time: 51 us -> 47.2 us (0.925)
  Pallas kernels: 48.9 us -> 45.1 us
    pallas_call x1, Pallas kernels: 48.9 us -> 45.1 us  [shards(): pl.pallas_call(kernel, out_shape=(pltpu.VMEM((3, NAT, 128), F32), pltpu.V...]
where the time goes in v4:
time: 47.2 us; the launch traced here: 47.1 us
  Pallas kernels  45.1 us (96%)
  local copies, waits for them, and re-layouts  1.37 us (3%)
  between operations  0.64 us (1%)
    pallas_call x1, Pallas kernels, shards(): pl.pallas_call(kernel, out_shape=(pltpu.VMEM((3, NAT, 128), F32), pltpu.V...  45.1 us
    unnamed x2, local copies, waits for them, and re-layouts  1.37 us

profile of v4, /device:TPU:1, one launch (start us, length us, event | category | flops | bytes accessed | tf_op | source)
XLA Modules:
  0.0 47.1 jit_solution(15699675863404062260)
XLA Ops:
  0.6 45.1 %shard_map.248 = (f32[3,216,128]{2,1,0:T(8,128)S(1)}, f32[216,128]{1,0:T(8,128)S(1)}) custom-call(f32[3,216,128]{2,1,0:T(8,128)} %refs_0_.1, f32[3,216,128]{2,1,0:T(8,128)} %refs_1_.1, f32[216,128]{1,0:T(8,128)} %refs_2_.1, s32[1,128]{1,0:T(1,128)} %refs_3_.1, f32[256,256]{1,0:T(8,128)} %refs_4_.1, bf16[672,256]{1,0:T(8,128)(2,1)} %constant.40.clone.refs_5_, ...), custom_call_target="tpu_custom_call" | custom-call | tf_op jit(solution)/shard_map/pallas_call | solution.py:829
  45.7 0.7 %copy.29 = f32[3,216,128]{2,1,0:T(8,128)} copy(f32[3,216,128]{2,1,0:T(8,128)S(1)} %get-tuple-element.2) | data formatting | bytes 663552
  46.4 0.6 %copy.30 = f32[216,128]{1,0:T(8,128)} copy(f32[216,128]{1,0:T(8,128)S(1)} %get-tuple-element.3) | data formatting | bytes 221184
